TPU v7x, 32 devices: a whole 2x2x4 slice. The times are simulated.
32 devices in a mesh: runs: 2 (over y), horiz: 4 (over z), comp: 2 (over x), vert: 2 (over core).
Axes of the slice: x: 2, y: 2, z: 4, core: 2. Of those that a mesh axis runs over, the one named last changes fastest.
Arguments:
- atm_state: float32 [128, 128, 512], P('vert', ('runs', 'comp'), 'horiz'), parts along dimension 1, may hold values from -6 to 6
- atm_coeffs: float32 [4, 128], P(None, 'vert'), may hold values from 0.02 to 0.25, as said below
- ocean_state: float32 [80, 64, 512], P('vert', ('runs', 'comp'), 'horiz'), parts along dimension 1, may hold values from -6 to 6
- ocean_coeffs: float32 [4, 80], P(None, 'vert'), may hold values from 0.02 to 0.25, as said below
- atm_flux: bfloat16 [8, 256, 128], P('vert', ('runs', 'horiz', 'comp')), parts along dimension 1, may hold values from -6 to 6
- remap_weights: bfloat16 [32, 128, 128], replicated, may hold values from -0.5 to 0.5
- remap_list: int32 [8, 8, 3], replicated, may hold values from 0 to 127, as said below
- ocean_mask: int32 [64, 128], P(('horiz', 'comp')), may hold values 0 or 1
Outputs:
- atm_final: float32 [128, 128, 512], P('vert', ('runs', 'comp'), 'horiz'), parts along dimension 1
- ocean_final: float32 [80, 64, 512], P('vert', ('runs', 'comp'), 'horiz'), parts along dimension 1
- remapped: float32 [8, 128, 128], P('vert', ('runs', 'horiz', 'comp')), parts along dimension 1
There are 2 independent parts, one for each index of `runs`. A program takes and returns all parts, laid end to end along the dimension named above; an argument that names none is the same for every part. Nothing has to cross between parts.
Inputs may be any that keep to these rules, and one draw needn't show every extreme that they name: `remap_list`: row p lists the entries whose destination blocks are p * 8 to (p + 1) * 8 - 1. In every row at most 2 entries have source blocks of one device (blocks d * 16 to (d + 1) * 16 - 1), and in every row some device has exactly 2. Weight block indices lie in 0 to 31. `atm_coeffs`: row 0 and row 1 lie in 0.05 to 0.25, row 2 in 0.02 to 0.08, row 3 in 0.03 to 0.15. `ocean_coeffs`: row 0 and row 1 lie in 0.05 to 0.25, row 2 in 0.02 to 0.08, row 3 in 0.03 to 0.15.
All inputs are finite; a program needn't handle non-finite values. No bound on the sum of `ocean_mask` on one device may be relied on, other than what follows from the above.
Results may differ from a plain program's by a relative error of at most 0.0003.
Values may be sent and summed in bfloat16 or wider, within the bound.
A program may use at most 64 MiB of HBM per device.

v0:
```python
import jax
import jax.numpy as jnp
from jax import lax
from jax.sharding import PartitionSpec as P

LEV_A = 128
LEV_O = 80
STEPS = 4
CAP = 2


def padded_2(cells, sides, width):
    for axis, dim in sides:
        count = lax.axis_size(axis)
        head = lax.slice_in_dim(cells, 0, width, axis=dim)
        tail = lax.slice_in_dim(cells, cells.shape[dim] - width, cells.shape[dim], axis=dim)
        cells = jnp.concatenate(
            [
                lax.ppermute(tail, axis, [(i, (i + 1) % count) for i in range(count)]),
                cells,
                lax.ppermute(head, axis, [((i + 1) % count, i) for i in range(count)]),
            ],
            axis=dim,
        )
    return cells


def advance(padded, coeffs, column_mean):
    middle = padded[:, 1:-1, 1:-1]
    west_side = padded[:, 1:-1, :-2]
    east_side = padded[:, 1:-1, 2:]
    south_side = padded[:, :-2, 1:-1]
    north_side = padded[:, 2:, 1:-1]
    courant_x = coeffs[0][:, None, None]
    courant_y = coeffs[1][:, None, None]
    diffusion = coeffs[2][:, None, None]
    mixing = coeffs[3][:, None, None]
    return (
        middle
        - courant_x * (middle - west_side)
        - courant_y * (middle - south_side)
        + diffusion * (east_side + west_side + north_side + south_side - 4.0 * middle)
        - mixing * (middle - column_mean[None])
    )


def column_totals(atm_field, ocean_field):
    return (
        lax.psum(jnp.sum(atm_field, axis=0).astype(jnp.bfloat16), "vert").astype(jnp.float32),
        lax.psum(jnp.sum(ocean_field, axis=0).astype(jnp.bfloat16), "vert").astype(jnp.float32),
    )


def remap_fluxes(atm_flux, remap_weights, remap_list, ocean_mask):
    peer_count = lax.axis_size(("horiz", "comp"))
    own_index = lax.axis_index(("horiz", "comp"))
    flux_local = atm_flux.shape[0]
    nba_local = atm_flux.shape[1]
    block_cells = atm_flux.shape[2]
    nbo_local = ocean_mask.shape[0]
    entries = remap_list.shape[1]
    source = remap_list[:, :, 0]
    source_device = source // nba_local
    source_local = source % nba_local
    earlier = (
        jnp.arange(entries, dtype=jnp.int32)[None, :]
        < jnp.arange(entries, dtype=jnp.int32)[:, None]
    )
    same_source = source_device[:, :, None] == source_device[:, None, :]
    arrival_rank = jnp.sum((same_source & earlier[None]).astype(jnp.int32), axis=2)
    from_here = source_device == own_index
    slot_hot = (
        (arrival_rank[:, :, None] == jnp.arange(CAP, dtype=jnp.int32)) & from_here[:, :, None]
    ).astype(jnp.bfloat16)
    block_hot = (source_local[:, :, None] == jnp.arange(nba_local, dtype=jnp.int32)).astype(
        jnp.bfloat16
    )
    selection = jnp.einsum(
        "pec,peb->pcb", slot_hot, block_hot, preferred_element_type=jnp.float32
    ).astype(jnp.bfloat16)
    outgoing = jnp.einsum(
        "pcb,fbk->pcfk", selection, atm_flux, preferred_element_type=jnp.float32
    ).astype(jnp.bfloat16)
    incoming = lax.all_to_all(outgoing, ("horiz", "comp"), split_axis=0, concat_axis=0, tiled=True)
    flat_slots = incoming.reshape(peer_count * CAP, flux_local, block_cells)
    own_list = lax.dynamic_index_in_dim(remap_list, own_index, 0, keepdims=False)
    own_rank = lax.dynamic_index_in_dim(arrival_rank, own_index, 0, keepdims=False)
    slot_index = own_list[:, 0] // nba_local * CAP + own_rank
    arriving = jnp.take(flat_slots, slot_index, axis=0)
    weights = jnp.take(remap_weights, own_list[:, 2], axis=0)
    products = jnp.einsum("efi,eij->efj", arriving, weights, preferred_element_type=jnp.float32)
    target = own_list[:, 1] % nbo_local
    dest_hot = (target[None, :] == jnp.arange(nbo_local, dtype=jnp.int32)[:, None]).astype(
        jnp.float32
    )
    summed = jnp.einsum("oe,efj->foj", dest_hot, products, precision=lax.Precision.HIGHEST)
    return summed * ocean_mask.astype(jnp.float32)[None]


def body(
    atm_state,
    atm_coeffs,
    ocean_state,
    ocean_coeffs,
    atm_flux,
    remap_weights,
    remap_list,
    ocean_mask,
):
    remapped = remap_fluxes(atm_flux, remap_weights, remap_list, ocean_mask)
    atm_field = atm_state
    ocean_field = ocean_state
    for iteration in range(STEPS):
        atm_sums, ocean_sums = column_totals(atm_field, ocean_field)
        atm_padded = padded_2(atm_field, (("horiz", 2), ("comp", 1)), 1)
        ocean_padded = padded_2(ocean_field, (("horiz", 2), ("comp", 1)), 1)
        atm_field = advance(atm_padded, atm_coeffs, atm_sums / LEV_A)
        ocean_field = advance(ocean_padded, ocean_coeffs, ocean_sums / LEV_O)
    return (atm_field, ocean_field, remapped)


def solution(mesh):
    return jax.shard_map(
        body,
        mesh=mesh,
        in_specs=(
            P("vert", ("runs", "comp"), "horiz"),
            P(None, "vert"),
            P("vert", ("runs", "comp"), "horiz"),
            P(None, "vert"),
            P("vert", ("runs", "horiz", "comp"), None),
            P(),
            P(),
            P(("horiz", "comp"), None),
        ),
        out_specs=(
            P("vert", ("runs", "comp"), "horiz"),
            P("vert", ("runs", "comp"), "horiz"),
            P("vert", ("runs", "horiz", "comp"), None),
        ),
        check_vma=False,
    )
```

profile of v0, /device:TPU:0, one launch (start us, length us, event | category | flops | bytes accessed | tf_op | source)
XLA Modules:
  0.0 175.1 jit_solution(15014529050885037683)
XLA Ops:
  0.6 2.0 %fusion.149 = (f32[64,32,1]{2,1,0:T(8,128)S(1)}, f32[64,32,1]{2,1,0:T(8,128)S(1)}) fusion(f32[64,32,128]{2,1,0:T(8,128)} %param.8), kind=kLoop, calls=%fused_computation.285 | loop fusion | bytes 32768 | tf_op jit(solution)/shard_map/slice | solution.py:16
  2.7 1.2 copy.114
  3.9 5.0 %collective-permute-start.1 = (f32[64,32,1]{0,1,2:T(8,128)}, f32[64,32,1]{0,1,2:T(8,128)}, u32[]{:S(2)}, u32[]{:S(2)}) collective-permute-start(f32[64,32,1]{0,1,2:T(8,128)} %copy.114), channel_id=1, source_target_pairs={{4,0},{8,4},{12,8},{0,12},{5,1},{9,5},{13,9},{1,13},{6,2},{10,6},{... | collective-permute-start | bytes 24584 | tf_op jit(solution)/shard_map/ppermute | solution.py:21
  8.9 1.2 copy.113
  11.0 3.8 %collective-permute-start.17 = (f32[40,16,1]{2,1,0:T(8,128)}, f32[40,16,1]{2,1,0:T(8,128)S(1)}, u32[]{:S(2)}, u32[]{:S(2)}) collective-permute-start(f32[40,16,1]{2,1,0:T(8,128)} %get-tuple-element.68), channel_id=1, source_target_pairs={{4,0},{8,4},{12,8},{0,12},{5,1},{9,5},{13,9},{1,13},{6,2},{10,6},{... | collective-permute-start | bytes 7688 | tf_op jit(solution)/shard_map/ppermute | solution.py:21
  16.6 6.0 %all-to-all-start = ((bf16[8,2,4,128]{3,2,1,0:T(4,128)(2,1)}), bf16[8,2,4,128]{3,2,1,0:T(4,128)(2,1)S(1)}, u32[]{:S(2)}, u32[]{:S(2)}) async-start(bf16[8,2,4,128]{3,2,1,0:T(4,128)(2,1)} %copy.103), calls=%async_computation | async-start | bytes 32768 | tf_op jit(solution)/shard_map/all_to_all | solution.py:84
  24.0 3.3 %all-reduce.3 = (bf16[32,128]{1,0:T(8,128)(2,1)S(1)}, bf16[16,128]{1,0:T(8,128)(2,1)S(1)}) all-reduce(bf16[32,128]{1,0:T(8,128)(2,1)S(1)} %reduce_sum.81, bf16[16,128]{1,0:T(8,128)(2,1)S(1)} %reduce_sum.85), channel_id=1, replica_groups=mesh['runs'=2,'horiz'=4,'comp'=2,'vert'=2] {'vert'}, use_global_device_ids=true, to_apply=%region_1.2 | all-reduce | flops 6144 | bytes 24576 | tf_op jit(solution)/shard_map/psum | solution.py:49
  31.4 2.0 %collective-permute-start.19 = (f32[40,1,130]{2,1,0:T(1,128)}, f32[40,1,130]{2,1,0:T(1,128)S(1)}, u32[]{:S(2)}, u32[]{:S(2)}) collective-permute-start(f32[40,1,130]{2,1,0:T(1,128)} %get-tuple-element.60), channel_id=1, source_target_pairs={{2,0},{0,2},{3,1},{1,3},{6,4},{4,6},{7,5},{5,7},{10,8},{8,10},{11,... | collective-permute-start | bytes 62408 | tf_op jit(solution)/shard_map/ppermute | solution.py:21
  35.4 1.4 gather_fusion.1
  36.8 1.1 copy.78
  37.9 2.1 %copy.71 = f32[64,32,1]{2,0,1:T(8,128)} copy(f32[64,32,1]{0,1,2:T(8,128)} %collective-permute-done) | data formatting | bytes 16384 | tf_op jit(solution)/shard_map/ppermute | solution.py:19
  40.8 2.7 %fusion.142 = (bf16[16,128]{1,0:T(8,128)(2,1)}, f32[40,16,128]{2,1,0:T(8,128)S(1)}) fusion(f32[40,16,128]{2,1,0:T(8,128)S(1)} %copy-done.11, f32[16,128]{1,0:T(8,128)S(1)} %convert_multiply_fusion.7, f32[40]{0:T(128)S(1)} %copy-done.33, f32[40,1,130]{2,1,0:T(1,128)S(1)} %collective-permute-done.19, f32[40,16,1]{2,1,0:T(8,128)} %copy-done.16, ...), kind=kLoop, calls=%fused_computation.280 | loop fusion | flops 2045952 | bytes 715008 | tf_op jit(solution)/shard_map/reduce_sum | solution.py:50
  43.6 3.8 %collective-permute-start.21 = (f32[40,16,1]{2,1,0:T(8,128)S(1)}, f32[40,16,1]{2,1,0:T(8,128)S(1)}, u32[]{:S(2)}, u32[]{:S(2)}) collective-permute-start(f32[40,16,1]{2,1,0:T(8,128)S(1)} %get-tuple-element.66), channel_id=1, source_target_pairs={{4,0},{8,4},{12,8},{0,12},{5,1},{9,5},{13,9},{1,13},{6,2},{10,6},{... | collective-permute-start | bytes 7688 | tf_op jit(solution)/shard_map/ppermute | solution.py:21
  47.6 1.5 collective-permute-start.3
  49.7 5.9 %collective-permute-done.21 = f32[40,16,1]{2,1,0:T(8,128)S(1)} collective-permute-done((f32[40,16,1]{2,1,0:T(8,128)S(1)}, f32[40,16,1]{2,1,0:T(8,128)S(1)}, u32[]{:S(2)}, u32[]{:S(2)}) %collective-permute-start.21) | collective-permute-done | bytes 2592 | tf_op jit(solution)/shard_map/ppermute | solution.py:21
  55.6 6.8 %collective-permute-done.20 = f32[40,16,1]{2,1,0:T(8,128)S(1)} collective-permute-done((f32[40,16,1]{2,1,0:T(8,128)S(1)}, f32[40,16,1]{2,1,0:T(8,128)S(1)}, u32[]{:S(2)}, u32[]{:S(2)}) %collective-permute-start.20) | collective-permute-done | bytes 2592 | tf_op jit(solution)/shard_map/ppermute | solution.py:19
  62.4 1.0 pad_maximum_fusion.84
  63.4 1.5 collective-permute-start.23
  68.9 3.8 %fusion.144 = (bf16[32,128]{1,0:T(8,128)(2,1)S(1)}, f32[64,32,128]{2,0,1:T(8,128)S(1)}) fusion(f32[64,32,128]{2,0,1:T(8,128)S(1)} %copy.74, f32[32,128]{1,0:T(8,128)S(1)} %convert_multiply_fusion.3, f32[64]{0:T(128)S(1)} %copy-done.49, f32[64,1,130]{2,0,1:T(8,128)S(1)} %collective-permute-done.3, f32[64,32,1]{2,0,1:T(8,128)} %copy-done.2, ...), kind=kLoop, calls=%fused_computation.281 | loop fusion | flops 6549504 | bytes 2205696 | tf_op jit(solution)/shard_map/reduce_sum | solution.py:49
  72.6 3.3 %all-reduce.2 = (bf16[32,128]{1,0:T(8,128)(2,1)S(1)}, bf16[16,128]{1,0:T(8,128)(2,1)S(1)}) all-reduce(bf16[32,128]{1,0:T(8,128)(2,1)S(1)} %get-tuple-element.35, bf16[16,128]{1,0:T(8,128)(2,1)S(1)} %copy-done.23), channel_id=1, replica_groups=mesh['runs'=2,'horiz'=4,'comp'=2,'vert'=2] {'vert'}, use_global_device_ids=true, to_apply=%region_3.4 | all-reduce | flops 6144 | bytes 24576 | tf_op jit(solution)/shard_map/psum | solution.py:49
  75.9 1.3 fusion.148
  77.3 1.6 copy.86
  78.9 1.8 %collective-permute-start.5 = (f32[64,32,1]{0,1,2:T(8,128)S(1)}, f32[64,32,1]{0,1,2:T(8,128)}, u32[]{:S(2)}, u32[]{:S(2)}) collective-permute-start(f32[64,32,1]{0,1,2:T(8,128)S(1)} %copy.86), channel_id=1, source_target_pairs={{4,0},{8,4},{12,8},{0,12},{5,1},{9,5},{13,9},{1,13},{6,2},{10,6},{... | collective-permute-start | bytes 24584 | tf_op jit(solution)/shard_map/ppermute | solution.py:21
  80.6 1.0 copy.84
  82.6 2.2 %fusion.138 = (bf16[16,128]{1,0:T(8,128)(2,1)S(1)}, f32[40,16,128]{2,1,0:T(8,128)S(1)}) fusion(f32[40,16,128]{2,1,0:T(8,128)S(1)} %copy-done.13, f32[16,128]{1,0:T(8,128)S(1)} %convert_multiply_fusion.6, f32[40]{0:T(128)S(1)} %copy-done.34, f32[40,1,130]{2,1,0:T(1,128)S(1)} %collective-permute-done.23, f32[40,16,1]{2,1,0:T(8,128)} %copy-done.18, ...), kind=kLoop, calls=%fused_computation.278 | loop fusion | flops 2045952 | bytes 715008 | tf_op jit(solution)/shard_map/reduce_sum | solution.py:50
  85.7 3.5 %collective-permute-start.25 = (f32[40,16,1]{2,1,0:T(8,128)}, f32[40,16,1]{2,1,0:T(8,128)}, u32[]{:S(2)}, u32[]{:S(2)}) collective-permute-start(f32[40,16,1]{2,1,0:T(8,128)} %get-tuple-element.64), channel_id=1, source_target_pairs={{4,0},{8,4},{12,8},{0,12},{5,1},{9,5},{13,9},{1,13},{6,2},{10,6},{... | collective-permute-start | bytes 7688 | tf_op jit(solution)/shard_map/ppermute | solution.py:21
  89.3 1.1 copy.88
  90.4 2.1 %copy.85 = f32[64,32,1]{2,0,1:T(8,128)} copy(f32[64,32,1]{0,1,2:T(8,128)} %collective-permute-done.4) | data formatting | bytes 16384 | tf_op jit(solution)/shard_map/ppermute | solution.py:19
  92.5 1.0 pad_maximum_fusion.72
  93.5 1.5 collective-permute-start.7
  95.6 2.1 %collective-permute-done.25 = f32[40,16,1]{2,1,0:T(8,128)} collective-permute-done((f32[40,16,1]{2,1,0:T(8,128)}, f32[40,16,1]{2,1,0:T(8,128)}, u32[]{:S(2)}, u32[]{:S(2)}) %collective-permute-start.25) | collective-permute-done | bytes 2592 | tf_op jit(solution)/shard_map/ppermute | solution.py:21
  97.7 6.6 %collective-permute-done.24 = f32[40,16,1]{2,1,0:T(8,128)} collective-permute-done((f32[40,16,1]{2,1,0:T(8,128)}, f32[40,16,1]{2,1,0:T(8,128)}, u32[]{:S(2)}, u32[]{:S(2)}) %collective-permute-start.24) | collective-permute-done | bytes 2592 | tf_op jit(solution)/shard_map/ppermute | solution.py:19
  104.2 2.1 %pad_maximum_fusion.81 = (f32[40,1,130]{2,1,0:T(1,128)}, f32[40,1,130]{2,1,0:T(1,128)}) fusion(f32[40,16,1]{2,1,0:T(8,128)} %collective-permute-done.25, f32[40,16,128]{2,1,0:T(8,128)S(1)} %get-tuple-element.30, f32[40,16,1]{2,1,0:T(8,128)} %collective-permute-done.24), kind=kLoop, calls=%fused_computation.196 | loop fusion | flops 20800 | bytes 374400 | tf_op jit(solution)/shard_map/slice | solution.py:16
  106.4 1.5 collective-permute-start.27
  108.5 1.5 fusion.140
  110.1 1.4 fusion.147
  111.8 1.8 %collective-permute-start.9 = (f32[64,32,1]{0,1,2:T(8,128)S(1)}, f32[64,32,1]{0,1,2:T(8,128)}, u32[]{:S(2)}, u32[]{:S(2)}) collective-permute-start(f32[64,32,1]{0,1,2:T(8,128)S(1)} %copy.92), channel_id=1, source_target_pairs={{4,0},{8,4},{12,8},{0,12},{5,1},{9,5},{13,9},{1,13},{6,2},{10,6},{... | collective-permute-start | bytes 24584 | tf_op jit(solution)/shard_map/ppermute | solution.py:21
  113.6 2.2 %copy.90 = f32[64,32,1]{0,1,2:T(8,128)} copy(f32[64,32,1]{2,0,1:T(8,128)} %get-tuple-element.47) | data formatting | bytes 16384 | tf_op jit(solution)/shard_map/slice | solution.py:16
  116.1 3.3 %all-reduce.1 = (bf16[32,128]{1,0:T(8,128)(2,1)S(1)}, bf16[16,128]{1,0:T(8,128)(2,1)S(1)}) all-reduce(bf16[32,128]{1,0:T(8,128)(2,1)S(1)} %get-tuple-element.31, bf16[16,128]{1,0:T(8,128)(2,1)S(1)} %get-tuple-element.29), channel_id=1, replica_groups=mesh['runs'=2,'horiz'=4,'comp'=2,'vert'=2] {'vert'}, use_global_device_ids=true, to_apply=%region_5.6 | all-reduce | flops 6144 | bytes 24576 | tf_op jit(solution)/shard_map/psum | solution.py:49
  120.0 2.8 %fusion.134 = (bf16[16,128]{1,0:T(8,128)(2,1)}, f32[40,16,128]{2,1,0:T(8,128)S(1)}) fusion(f32[40,16,128]{2,1,0:T(8,128)S(1)} %copy-done.15, f32[16,128]{1,0:T(8,128)S(1)} %convert_multiply_fusion.5, f32[40]{0:T(128)S(1)} %copy-done.35, f32[40,1,130]{2,1,0:T(1,128)S(1)} %collective-permute-done.27, f32[40,16,1]{2,1,0:T(8,128)} %collective-permute-done.25, ...), kind=kLoop, calls=%fused_computation.276 | loop fusion | flops 2045952 | bytes 715008 | tf_op jit(solution)/shard_map/reduce_sum | solution.py:50
  123.7 3.5 %collective-permute-start.29 = (f32[40,16,1]{2,1,0:T(8,128)}, f32[40,16,1]{2,1,0:T(8,128)}, u32[]{:S(2)}, u32[]{:S(2)}) collective-permute-start(f32[40,16,1]{2,1,0:T(8,128)} %get-tuple-element.62), channel_id=1, source_target_pairs={{4,0},{8,4},{12,8},{0,12},{5,1},{9,5},{13,9},{1,13},{6,2},{10,6},{... | collective-permute-start | bytes 7688 | tf_op jit(solution)/shard_map/ppermute | solution.py:21
  127.2 1.1 copy.94
  128.4 2.1 %copy.91 = f32[64,32,1]{2,0,1:T(8,128)} copy(f32[64,32,1]{0,1,2:T(8,128)} %collective-permute-done.8) | data formatting | bytes 16384 | tf_op jit(solution)/shard_map/ppermute | solution.py:19
  130.5 1.0 pad_maximum_fusion.69
  131.5 1.5 collective-permute-start.11
  133.6 2.0 %collective-permute-done.29 = f32[40,16,1]{2,1,0:T(8,128)} collective-permute-done((f32[40,16,1]{2,1,0:T(8,128)}, f32[40,16,1]{2,1,0:T(8,128)}, u32[]{:S(2)}, u32[]{:S(2)}) %collective-permute-start.29) | collective-permute-done | bytes 2592 | tf_op jit(solution)/shard_map/ppermute | solution.py:21
  135.6 7.1 %collective-permute-done.28 = f32[40,16,1]{2,1,0:T(8,128)} collective-permute-done((f32[40,16,1]{2,1,0:T(8,128)}, f32[40,16,1]{2,1,0:T(8,128)}, u32[]{:S(2)}, u32[]{:S(2)}) %collective-permute-start.28) | collective-permute-done | bytes 2592 | tf_op jit(solution)/shard_map/ppermute | solution.py:19
  142.8 2.1 %pad_maximum_fusion.78 = (f32[40,1,130]{2,1,0:T(1,128)}, f32[40,1,130]{2,1,0:T(1,128)}) fusion(f32[40,16,1]{2,1,0:T(8,128)} %collective-permute-done.29, f32[40,16,128]{2,1,0:T(8,128)S(1)} %get-tuple-element.26, f32[40,16,1]{2,1,0:T(8,128)} %collective-permute-done.28), kind=kLoop, calls=%fused_computation.193 | loop fusion | flops 20800 | bytes 374400 | tf_op jit(solution)/shard_map/slice | solution.py:16
  144.9 1.5 collective-permute-start.31
  147.1 1.5 fusion.136
  148.6 1.3 fusion.146
  149.9 1.6 copy.98
  151.5 1.8 %collective-permute-start.13 = (f32[64,32,1]{0,1,2:T(8,128)S(1)}, f32[64,32,1]{0,1,2:T(8,128)}, u32[]{:S(2)}, u32[]{:S(2)}) collective-permute-start(f32[64,32,1]{0,1,2:T(8,128)S(1)} %copy.98), channel_id=1, source_target_pairs={{4,0},{8,4},{12,8},{0,12},{5,1},{9,5},{13,9},{1,13},{6,2},{10,6},{... | collective-permute-start | bytes 24584 | tf_op jit(solution)/shard_map/ppermute | solution.py:21
  153.3 1.0 copy.96
  154.5 3.9 %all-reduce = (bf16[32,128]{1,0:T(8,128)(2,1)}, bf16[16,128]{1,0:T(8,128)(2,1)S(1)}) all-reduce(bf16[32,128]{1,0:T(8,128)(2,1)S(1)} %get-tuple-element.27, bf16[16,128]{1,0:T(8,128)(2,1)S(1)} %copy-done.22), channel_id=1, replica_groups=mesh['runs'=2,'horiz'=4,'comp'=2,'vert'=2] {'vert'}, use_global_device_ids=true, to_apply=%region_7.8 | all-reduce | flops 6144 | bytes 24576 | tf_op jit(solution)/shard_map/psum | solution.py:49
  159.1 2.9 %fusion.59 = f32[40,16,128]{2,1,0:T(8,128)} fusion(f32[40,1,130]{2,1,0:T(1,128)S(1)} %collective-permute-done.31, f32[40,16,1]{2,1,0:T(8,128)} %collective-permute-done.29, f32[40,16,128]{2,1,0:T(8,128)S(1)} %get-tuple-element.26, f32[40,16,1]{2,1,0:T(8,128)} %collective-permute-done.28, f32[40,1,130]{2,1,0:T(1,128)} %collective-permute-done.30, ...), kind=kLoop, calls=%fused_computation.97 | loop fusion | flops 1966080 | bytes 710912 | tf_op jit(solution)/shard_map/sub | solution.py:39
  162.0 1.1 copy.100
  163.1 2.1 %copy.97 = f32[64,32,1]{2,0,1:T(8,128)} copy(f32[64,32,1]{0,1,2:T(8,128)} %collective-permute-done.12) | data formatting | bytes 16384 | tf_op jit(solution)/shard_map/ppermute | solution.py:19
  165.2 1.0 pad_maximum_fusion.66
  166.2 1.5 collective-permute-start.15
  168.3 2.6 %collective-permute-done.15 = f32[64,1,130]{2,0,1:T(8,128)S(1)} collective-permute-done((f32[64,1,130]{2,0,1:T(8,128)S(1)}, f32[64,1,130]{2,0,1:T(8,128)S(1)}, u32[]{:S(2)}, u32[]{:S(2)}) %collective-permute-start.15) | collective-permute-done | bytes 33312 | tf_op jit(solution)/shard_map/ppermute | solution.py:21
  170.9 1.1 collective-permute-done.14
  172.0 1.5 fusion.7
  173.6 1.6 copy.107
  (209 shorter events, 23.4 us)
Async XLA Ops:
  0.6 34.8 %copy-start = (bf16[32,128,128]{2,1,0:T(8,128)(2,1)S(1)}, bf16[32,128,128]{2,1,0:T(8,128)(2,1)}, u32[]{:S(2)}) copy-start(bf16[32,128,128]{2,1,0:T(8,128)(2,1)} %param.13) | copy-start | bytes 3145732
  3.9 32.9 %collective-permute-start.1 = (f32[64,32,1]{0,1,2:T(8,128)}, f32[64,32,1]{0,1,2:T(8,128)}, u32[]{:S(2)}, u32[]{:S(2)}) collective-permute-start(f32[64,32,1]{0,1,2:T(8,128)} %copy.114), channel_id=1, source_target_pairs={{4,0},{8,4},{12,8},{0,12},{5,1},{9,5},{13,9},{1,13},{6,2},{10,6},{... | collective-permute-start | bytes 24584 | tf_op jit(solution)/shard_map/ppermute | solution.py:21
  8.9 13.7 %copy-start.1 = (f32[64,32,128]{2,1,0:T(8,128)S(1)}, f32[64,32,128]{2,1,0:T(8,128)}, u32[]{:S(2)}) copy-start(f32[64,32,128]{2,1,0:T(8,128)} %param.8) | copy-start | bytes 3145732
  10.1 4.7 %copy-start.21 = (s32[8,8,3]{1,0,2:T(8,128)S(1)}, s32[8,8,3]{1,0,2:T(8,128)}, u32[]{:S(2)}) copy-start(s32[8,8,3]{1,0,2:T(8,128)} %param.14) | copy-start | bytes 2308
  10.2 27.8 %collective-permute-start = (f32[64,32,1]{0,1,2:T(8,128)}, f32[64,32,1]{0,1,2:T(8,128)}, u32[]{:S(2)}, u32[]{:S(2)}) collective-permute-start(f32[64,32,1]{0,1,2:T(8,128)} %copy.113), channel_id=1, source_target_pairs={{0,4},{4,8},{8,12},{12,0},{1,5},{5,9},{9,13},{13,1},{2,6},{6,10},{... | collective-permute-start | bytes 24584 | tf_op jit(solution)/shard_map/ppermute | solution.py:19
  11.0 19.5 %collective-permute-start.17 = (f32[40,16,1]{2,1,0:T(8,128)}, f32[40,16,1]{2,1,0:T(8,128)S(1)}, u32[]{:S(2)}, u32[]{:S(2)}) collective-permute-start(f32[40,16,1]{2,1,0:T(8,128)} %get-tuple-element.68), channel_id=1, source_target_pairs={{4,0},{8,4},{12,8},{0,12},{5,1},{9,5},{13,9},{1,13},{6,2},{10,6},{... | collective-permute-start | bytes 7688 | tf_op jit(solution)/shard_map/ppermute | solution.py:21
  14.8 15.7 %collective-permute-start.16 = (f32[40,16,1]{2,1,0:T(8,128)S(1)}, f32[40,16,1]{2,1,0:T(8,128)S(1)}, u32[]{:S(2)}, u32[]{:S(2)}) collective-permute-start(f32[40,16,1]{2,1,0:T(8,128)S(1)} %get-tuple-element.67), channel_id=1, source_target_pairs={{0,4},{4,8},{8,12},{12,0},{1,5},{5,9},{9,13},{13,1},{2,6},{6,10},{... | collective-permute-start | bytes 7688 | tf_op jit(solution)/shard_map/ppermute | solution.py:19
  16.6 48.8 %all-to-all-start = ((bf16[8,2,4,128]{3,2,1,0:T(4,128)(2,1)}), bf16[8,2,4,128]{3,2,1,0:T(4,128)(2,1)S(1)}, u32[]{:S(2)}, u32[]{:S(2)}) async-start(bf16[8,2,4,128]{3,2,1,0:T(4,128)(2,1)} %copy.103), calls=%async_computation | async-start | bytes 32768 | tf_op jit(solution)/shard_map/all_to_all | solution.py:84
  31.4 8.6 %collective-permute-start.19 = (f32[40,1,130]{2,1,0:T(1,128)}, f32[40,1,130]{2,1,0:T(1,128)S(1)}, u32[]{:S(2)}, u32[]{:S(2)}) collective-permute-start(f32[40,1,130]{2,1,0:T(1,128)} %get-tuple-element.60), channel_id=1, source_target_pairs={{2,0},{0,2},{3,1},{1,3},{6,4},{4,6},{7,5},{5,7},{10,8},{8,10},{11,... | collective-permute-start | bytes 62408 | tf_op jit(solution)/shard_map/ppermute | solution.py:21
  33.4 6.6 %collective-permute-start.18 = (f32[40,1,130]{2,1,0:T(1,128)}, f32[40,1,130]{2,1,0:T(1,128)}, u32[]{:S(2)}, u32[]{:S(2)}) collective-permute-start(f32[40,1,130]{2,1,0:T(1,128)} %get-tuple-element.59), channel_id=1, source_target_pairs={{0,2},{2,0},{1,3},{3,1},{4,6},{6,4},{5,7},{7,5},{8,10},{10,8},{9,1... | collective-permute-start | bytes 62408 | tf_op jit(solution)/shard_map/ppermute | solution.py:19
  37.9 9.5 %copy-start.2 = (f32[64,32,1]{2,0,1:T(8,128)}, f32[64,32,1]{2,0,1:T(8,128)S(1)}, u32[]{:S(2)}) copy-start(f32[64,32,1]{2,0,1:T(8,128)S(1)} %copy.78) | copy-start | bytes 24580
  40.8 6.7 %copy-start.3 = (f32[64,32,1]{2,0,1:T(8,128)S(1)}, f32[64,32,1]{2,0,1:T(8,128)}, u32[]{:S(2)}) copy-start(f32[64,32,1]{2,0,1:T(8,128)} %copy.71) | copy-start | bytes 24580
  43.5 18.9 %copy-start.12 = (f32[40,16,128]{2,1,0:T(8,128)}, f32[40,16,128]{2,1,0:T(8,128)S(1)}, u32[]{:S(2)}) copy-start(f32[40,16,128]{2,1,0:T(8,128)S(1)} %get-tuple-element.34) | copy-start | bytes 983044
  43.6 11.9 %collective-permute-start.21 = (f32[40,16,1]{2,1,0:T(8,128)S(1)}, f32[40,16,1]{2,1,0:T(8,128)S(1)}, u32[]{:S(2)}, u32[]{:S(2)}) collective-permute-start(f32[40,16,1]{2,1,0:T(8,128)S(1)} %get-tuple-element.66), channel_id=1, source_target_pairs={{4,0},{8,4},{12,8},{0,12},{5,1},{9,5},{13,9},{1,13},{6,2},{10,6},{... | collective-permute-start | bytes 7688 | tf_op jit(solution)/shard_map/ppermute | solution.py:21
  47.4 15.0 %collective-permute-start.20 = (f32[40,16,1]{2,1,0:T(8,128)S(1)}, f32[40,16,1]{2,1,0:T(8,128)S(1)}, u32[]{:S(2)}, u32[]{:S(2)}) collective-permute-start(f32[40,16,1]{2,1,0:T(8,128)S(1)} %get-tuple-element.65), channel_id=1, source_target_pairs={{0,4},{4,8},{8,12},{12,0},{1,5},{5,9},{9,13},{13,1},{2,6},{6,10},{... | collective-permute-start | bytes 7688 | tf_op jit(solution)/shard_map/ppermute | solution.py:19
  47.6 20.6 %collective-permute-start.3 = (f32[64,1,130]{2,0,1:T(8,128)S(1)}, f32[64,1,130]{2,0,1:T(8,128)S(1)}, u32[]{:S(2)}, u32[]{:S(2)}) collective-permute-start(f32[64,1,130]{2,0,1:T(8,128)S(1)} %get-tuple-element.44), channel_id=1, source_target_pairs={{2,0},{0,2},{3,1},{1,3},{6,4},{4,6},{7,5},{5,7},{10,8},{8,10},{11,... | collective-permute-start | bytes 99848 | tf_op jit(solution)/shard_map/ppermute | solution.py:21
  49.1 17.0 %copy-start.20 = (bf16[8,128,128]{2,1,0:T(8,128)(2,1)S(1)}, bf16[8,128,128]{2,1,0:T(8,128)(2,1)}, u32[]{:S(2)}) copy-start(bf16[8,128,128]{2,1,0:T(8,128)(2,1)} %gather_fusion.1) | copy-start | bytes 786436
  49.1 19.1 %collective-permute-start.2 = (f32[64,1,130]{2,0,1:T(8,128)S(1)}, f32[64,1,130]{2,0,1:T(8,128)S(1)}, u32[]{:S(2)}, u32[]{:S(2)}) collective-permute-start(f32[64,1,130]{2,0,1:T(8,128)S(1)} %get-tuple-element.43), channel_id=1, source_target_pairs={{0,2},{2,0},{1,3},{3,1},{4,6},{6,4},{5,7},{7,5},{8,10},{10,8},{9,1... | collective-permute-start | bytes 99848 | tf_op jit(solution)/shard_map/ppermute | solution.py:19
  55.6 7.8 %copy-start.18 = (f32[40,16,1]{2,1,0:T(8,128)}, f32[40,16,1]{2,1,0:T(8,128)S(1)}, u32[]{:S(2)}) copy-start(f32[40,16,1]{2,1,0:T(8,128)S(1)} %collective-permute-done.21) | copy-start | bytes 7684
  63.4 18.5 %collective-permute-start.23 = (f32[40,1,130]{2,1,0:T(1,128)}, f32[40,1,130]{2,1,0:T(1,128)S(1)}, u32[]{:S(2)}, u32[]{:S(2)}) collective-permute-start(f32[40,1,130]{2,1,0:T(1,128)} %get-tuple-element.58), channel_id=1, source_target_pairs={{2,0},{0,2},{3,1},{1,3},{6,4},{4,6},{7,5},{5,7},{10,8},{8,10},{11,... | collective-permute-start | bytes 62408 | tf_op jit(solution)/shard_map/ppermute | solution.py:21
  64.8 17.1 %collective-permute-start.22 = (f32[40,1,130]{2,1,0:T(1,128)}, f32[40,1,130]{2,1,0:T(1,128)}, u32[]{:S(2)}, u32[]{:S(2)}) collective-permute-start(f32[40,1,130]{2,1,0:T(1,128)} %get-tuple-element.57), channel_id=1, source_target_pairs={{0,2},{2,0},{1,3},{3,1},{4,6},{6,4},{5,7},{7,5},{8,10},{10,8},{9,1... | collective-permute-start | bytes 62408 | tf_op jit(solution)/shard_map/ppermute | solution.py:19
  68.8 3.8 %copy-start.23 = (bf16[16,128]{1,0:T(8,128)(2,1)S(1)}, bf16[16,128]{1,0:T(8,128)(2,1)}, u32[]{:S(2)}) copy-start(bf16[16,128]{1,0:T(8,128)(2,1)} %get-tuple-element.33) | copy-start | bytes 12292
  78.9 10.4 %collective-permute-start.5 = (f32[64,32,1]{0,1,2:T(8,128)S(1)}, f32[64,32,1]{0,1,2:T(8,128)}, u32[]{:S(2)}, u32[]{:S(2)}) collective-permute-start(f32[64,32,1]{0,1,2:T(8,128)S(1)} %copy.86), channel_id=1, source_target_pairs={{4,0},{8,4},{12,8},{0,12},{5,1},{9,5},{13,9},{1,13},{6,2},{10,6},{... | collective-permute-start | bytes 24584 | tf_op jit(solution)/shard_map/ppermute | solution.py:21
  81.6 8.8 %collective-permute-start.4 = (f32[64,32,1]{0,1,2:T(8,128)}, f32[64,32,1]{0,1,2:T(8,128)}, u32[]{:S(2)}, u32[]{:S(2)}) collective-permute-start(f32[64,32,1]{0,1,2:T(8,128)} %copy.84), channel_id=1, source_target_pairs={{0,4},{4,8},{8,12},{12,0},{1,5},{5,9},{9,13},{13,1},{2,6},{6,10},{... | collective-permute-start | bytes 24584 | tf_op jit(solution)/shard_map/ppermute | solution.py:19
  84.7 19.5 %copy-start.14 = (f32[40,16,128]{2,1,0:T(8,128)}, f32[40,16,128]{2,1,0:T(8,128)S(1)}, u32[]{:S(2)}) copy-start(f32[40,16,128]{2,1,0:T(8,128)S(1)} %get-tuple-element.30) | copy-start | bytes 983044
  85.7 12.0 %collective-permute-start.25 = (f32[40,16,1]{2,1,0:T(8,128)}, f32[40,16,1]{2,1,0:T(8,128)}, u32[]{:S(2)}, u32[]{:S(2)}) collective-permute-start(f32[40,16,1]{2,1,0:T(8,128)} %get-tuple-element.64), channel_id=1, source_target_pairs={{4,0},{8,4},{12,8},{0,12},{5,1},{9,5},{13,9},{1,13},{6,2},{10,6},{... | collective-permute-start | bytes 7688 | tf_op jit(solution)/shard_map/ppermute | solution.py:21
  89.3 15.0 %collective-permute-start.24 = (f32[40,16,1]{2,1,0:T(8,128)}, f32[40,16,1]{2,1,0:T(8,128)}, u32[]{:S(2)}, u32[]{:S(2)}) collective-permute-start(f32[40,16,1]{2,1,0:T(8,128)} %get-tuple-element.63), channel_id=1, source_target_pairs={{0,4},{4,8},{8,12},{12,0},{1,5},{5,9},{9,13},{13,1},{2,6},{6,10},{... | collective-permute-start | bytes 7688 | tf_op jit(solution)/shard_map/ppermute | solution.py:19
  90.4 3.1 %copy-start.4 = (f32[64,32,1]{2,0,1:T(8,128)}, f32[64,32,1]{2,0,1:T(8,128)S(1)}, u32[]{:S(2)}) copy-start(f32[64,32,1]{2,0,1:T(8,128)S(1)} %copy.88) | copy-start | bytes 24580
  92.5 15.9 %copy-start.8 = (f32[64,32,1]{2,0,1:T(8,128)S(1)}, f32[64,32,1]{2,0,1:T(8,128)}, u32[]{:S(2)}) copy-start(f32[64,32,1]{2,0,1:T(8,128)} %copy.85) | copy-start | bytes 24580
  93.5 14.9 %copy-start.5 = (f32[64,32,1]{2,0,1:T(8,128)S(1)}, f32[64,32,1]{2,0,1:T(8,128)}, u32[]{:S(2)}) copy-start(f32[64,32,1]{2,0,1:T(8,128)} %copy-done.4) | copy-start | bytes 24580
  93.5 14.9 %collective-permute-start.7 = (f32[64,1,130]{2,0,1:T(8,128)S(1)}, f32[64,1,130]{2,0,1:T(8,128)S(1)}, u32[]{:S(2)}, u32[]{:S(2)}) collective-permute-start(f32[64,1,130]{2,0,1:T(8,128)S(1)} %get-tuple-element.42), channel_id=1, source_target_pairs={{2,0},{0,2},{3,1},{1,3},{6,4},{4,6},{7,5},{5,7},{10,8},{8,10},{11,... | collective-permute-start | bytes 99848 | tf_op jit(solution)/shard_map/ppermute | solution.py:21
  95.1 13.4 %collective-permute-start.6 = (f32[64,1,130]{2,0,1:T(8,128)S(1)}, f32[64,1,130]{2,0,1:T(8,128)S(1)}, u32[]{:S(2)}, u32[]{:S(2)}) collective-permute-start(f32[64,1,130]{2,0,1:T(8,128)S(1)} %get-tuple-element.41), channel_id=1, source_target_pairs={{0,2},{2,0},{1,3},{3,1},{4,6},{6,4},{5,7},{7,5},{8,10},{10,8},{9,1... | collective-permute-start | bytes 99848 | tf_op jit(solution)/shard_map/ppermute | solution.py:19
  106.4 2.1 %copy-start.54 = (f32[64]{0:T(128)S(1)}, f32[64]{0:T(128)}, u32[]{:S(2)}) copy-start(f32[64]{0:T(128)} %get-tuple-element.77) | copy-start | bytes 772
  106.4 2.1 %copy-start.42 = (f32[64]{0:T(128)S(1)}, f32[64]{0:T(128)}, u32[]{:S(2)}) copy-start(f32[64]{0:T(128)} %get-tuple-element.74) | copy-start | bytes 772
  106.4 2.2 %copy-start.46 = (f32[64]{0:T(128)S(1)}, f32[64]{0:T(128)}, u32[]{:S(2)}) copy-start(f32[64]{0:T(128)} %get-tuple-element.75) | copy-start | bytes 772
  106.4 2.2 %copy-start.50 = (f32[64]{0:T(128)S(1)}, f32[64]{0:T(128)}, u32[]{:S(2)}) copy-start(f32[64]{0:T(128)} %get-tuple-element.76) | copy-start | bytes 772
  106.4 13.0 %collective-permute-start.27 = (f32[40,1,130]{2,1,0:T(1,128)}, f32[40,1,130]{2,1,0:T(1,128)S(1)}, u32[]{:S(2)}, u32[]{:S(2)}) collective-permute-start(f32[40,1,130]{2,1,0:T(1,128)} %get-tuple-element.56), channel_id=1, source_target_pairs={{2,0},{0,2},{3,1},{1,3},{6,4},{4,6},{7,5},{5,7},{10,8},{8,10},{11,... | collective-permute-start | bytes 62408 | tf_op jit(solution)/shard_map/ppermute | solution.py:21
  107.9 11.5 %collective-permute-start.26 = (f32[40,1,130]{2,1,0:T(1,128)}, f32[40,1,130]{2,1,0:T(1,128)}, u32[]{:S(2)}, u32[]{:S(2)}) collective-permute-start(f32[40,1,130]{2,1,0:T(1,128)} %get-tuple-element.55), channel_id=1, source_target_pairs={{0,2},{2,0},{1,3},{3,1},{4,6},{6,4},{5,7},{7,5},{8,10},{10,8},{9,1... | collective-permute-start | bytes 62408 | tf_op jit(solution)/shard_map/ppermute | solution.py:19
  111.8 15.5 %collective-permute-start.9 = (f32[64,32,1]{0,1,2:T(8,128)S(1)}, f32[64,32,1]{0,1,2:T(8,128)}, u32[]{:S(2)}, u32[]{:S(2)}) collective-permute-start(f32[64,32,1]{0,1,2:T(8,128)S(1)} %copy.92), channel_id=1, source_target_pairs={{4,0},{8,4},{12,8},{0,12},{5,1},{9,5},{13,9},{1,13},{6,2},{10,6},{... | collective-permute-start | bytes 24584 | tf_op jit(solution)/shard_map/ppermute | solution.py:21
  113.5 5.9 %copy-start.15 = (f32[40,16,128]{2,1,0:T(8,128)S(1)}, f32[40,16,128]{2,1,0:T(8,128)}, u32[]{:S(2)}) copy-start(f32[40,16,128]{2,1,0:T(8,128)} %copy-done.14) | copy-start | bytes 983044
  115.8 12.6 %collective-permute-start.8 = (f32[64,32,1]{0,1,2:T(8,128)}, f32[64,32,1]{0,1,2:T(8,128)}, u32[]{:S(2)}, u32[]{:S(2)}) collective-permute-start(f32[64,32,1]{0,1,2:T(8,128)} %copy.90), channel_id=1, source_target_pairs={{0,4},{4,8},{8,12},{12,0},{1,5},{5,9},{9,13},{13,1},{2,6},{6,10},{... | collective-permute-start | bytes 24584 | tf_op jit(solution)/shard_map/ppermute | solution.py:19
  123.7 11.9 %collective-permute-start.29 = (f32[40,16,1]{2,1,0:T(8,128)}, f32[40,16,1]{2,1,0:T(8,128)}, u32[]{:S(2)}, u32[]{:S(2)}) collective-permute-start(f32[40,16,1]{2,1,0:T(8,128)} %get-tuple-element.62), channel_id=1, source_target_pairs={{4,0},{8,4},{12,8},{0,12},{5,1},{9,5},{13,9},{1,13},{6,2},{10,6},{... | collective-permute-start | bytes 7688 | tf_op jit(solution)/shard_map/ppermute | solution.py:21
  127.2 15.6 %collective-permute-start.28 = (f32[40,16,1]{2,1,0:T(8,128)}, f32[40,16,1]{2,1,0:T(8,128)}, u32[]{:S(2)}, u32[]{:S(2)}) collective-permute-start(f32[40,16,1]{2,1,0:T(8,128)} %get-tuple-element.61), channel_id=1, source_target_pairs={{0,4},{4,8},{8,12},{12,0},{1,5},{5,9},{9,13},{13,1},{2,6},{6,10},{... | collective-permute-start | bytes 7688 | tf_op jit(solution)/shard_map/ppermute | solution.py:19
  128.4 3.1 %copy-start.6 = (f32[64,32,1]{2,0,1:T(8,128)}, f32[64,32,1]{2,0,1:T(8,128)S(1)}, u32[]{:S(2)}) copy-start(f32[64,32,1]{2,0,1:T(8,128)S(1)} %copy.94) | copy-start | bytes 24580
  130.5 16.5 %copy-start.9 = (f32[64,32,1]{2,0,1:T(8,128)S(1)}, f32[64,32,1]{2,0,1:T(8,128)}, u32[]{:S(2)}) copy-start(f32[64,32,1]{2,0,1:T(8,128)} %copy.91) | copy-start | bytes 24580
  131.5 15.5 %copy-start.7 = (f32[64,32,1]{2,0,1:T(8,128)S(1)}, f32[64,32,1]{2,0,1:T(8,128)}, u32[]{:S(2)}) copy-start(f32[64,32,1]{2,0,1:T(8,128)} %copy-done.6) | copy-start | bytes 24580
  131.5 15.5 %collective-permute-start.11 = (f32[64,1,130]{2,0,1:T(8,128)S(1)}, f32[64,1,130]{2,0,1:T(8,128)S(1)}, u32[]{:S(2)}, u32[]{:S(2)}) collective-permute-start(f32[64,1,130]{2,0,1:T(8,128)S(1)} %get-tuple-element.40), channel_id=1, source_target_pairs={{2,0},{0,2},{3,1},{1,3},{6,4},{4,6},{7,5},{5,7},{10,8},{8,10},{11,... | collective-permute-start | bytes 99848 | tf_op jit(solution)/shard_map/ppermute | solution.py:21
  133.1 13.9 %collective-permute-start.10 = (f32[64,1,130]{2,0,1:T(8,128)S(1)}, f32[64,1,130]{2,0,1:T(8,128)S(1)}, u32[]{:S(2)}, u32[]{:S(2)}) collective-permute-start(f32[64,1,130]{2,0,1:T(8,128)S(1)} %get-tuple-element.39), channel_id=1, source_target_pairs={{0,2},{2,0},{1,3},{3,1},{4,6},{6,4},{5,7},{7,5},{8,10},{10,8},{9,1... | collective-permute-start | bytes 99848 | tf_op jit(solution)/shard_map/ppermute | solution.py:19
  144.9 2.1 %copy-start.55 = (f32[64]{0:T(128)S(1)}, f32[64]{0:T(128)}, u32[]{:S(2)}) copy-start(f32[64]{0:T(128)} %get-tuple-element.77) | copy-start | bytes 772
  144.9 2.1 %copy-start.43 = (f32[64]{0:T(128)S(1)}, f32[64]{0:T(128)}, u32[]{:S(2)}) copy-start(f32[64]{0:T(128)} %get-tuple-element.74) | copy-start | bytes 772
  144.9 2.2 %copy-start.47 = (f32[64]{0:T(128)S(1)}, f32[64]{0:T(128)}, u32[]{:S(2)}) copy-start(f32[64]{0:T(128)} %get-tuple-element.75) | copy-start | bytes 772
  144.9 2.2 %copy-start.51 = (f32[64]{0:T(128)S(1)}, f32[64]{0:T(128)}, u32[]{:S(2)}) copy-start(f32[64]{0:T(128)} %get-tuple-element.76) | copy-start | bytes 772
  144.9 13.5 %collective-permute-start.31 = (f32[40,1,130]{2,1,0:T(1,128)}, f32[40,1,130]{2,1,0:T(1,128)S(1)}, u32[]{:S(2)}, u32[]{:S(2)}) collective-permute-start(f32[40,1,130]{2,1,0:T(1,128)} %get-tuple-element.54), channel_id=1, source_target_pairs={{2,0},{0,2},{3,1},{1,3},{6,4},{4,6},{7,5},{5,7},{10,8},{8,10},{11,... | collective-permute-start | bytes 62408 | tf_op jit(solution)/shard_map/ppermute | solution.py:21
  146.4 12.0 %collective-permute-start.30 = (f32[40,1,130]{2,1,0:T(1,128)}, f32[40,1,130]{2,1,0:T(1,128)}, u32[]{:S(2)}, u32[]{:S(2)}) collective-permute-start(f32[40,1,130]{2,1,0:T(1,128)} %get-tuple-element.53), channel_id=1, source_target_pairs={{0,2},{2,0},{1,3},{3,1},{4,6},{6,4},{5,7},{7,5},{8,10},{10,8},{9,1... | collective-permute-start | bytes 62408 | tf_op jit(solution)/shard_map/ppermute | solution.py:19
  151.5 10.5 %collective-permute-start.13 = (f32[64,32,1]{0,1,2:T(8,128)S(1)}, f32[64,32,1]{0,1,2:T(8,128)}, u32[]{:S(2)}, u32[]{:S(2)}) collective-permute-start(f32[64,32,1]{0,1,2:T(8,128)S(1)} %copy.98), channel_id=1, source_target_pairs={{4,0},{8,4},{12,8},{0,12},{5,1},{9,5},{13,9},{1,13},{6,2},{10,6},{... | collective-permute-start | bytes 24584 | tf_op jit(solution)/shard_map/ppermute | solution.py:21
  154.3 8.8 %collective-permute-start.12 = (f32[64,32,1]{0,1,2:T(8,128)}, f32[64,32,1]{0,1,2:T(8,128)}, u32[]{:S(2)}, u32[]{:S(2)}) collective-permute-start(f32[64,32,1]{0,1,2:T(8,128)} %copy.96), channel_id=1, source_target_pairs={{0,4},{4,8},{8,12},{12,0},{1,5},{5,9},{9,13},{13,1},{2,6},{6,10},{... | collective-permute-start | bytes 24584 | tf_op jit(solution)/shard_map/ppermute | solution.py:19
  165.2 3.1 %copy-start.57 = (bf16[32,128]{1,0:T(8,128)(2,1)S(1)}, bf16[32,128]{1,0:T(8,128)(2,1)}, u32[]{:S(2)}) copy-start(bf16[32,128]{1,0:T(8,128)(2,1)} %get-tuple-element.12) | copy-start | bytes 24580
  165.2 6.8 %copy-start.10 = (f32[64,32,1]{2,0,1:T(8,128)S(1)}, f32[64,32,1]{2,0,1:T(8,128)}, u32[]{:S(2)}) copy-start(f32[64,32,1]{2,0,1:T(8,128)} %copy.97) | copy-start | bytes 24580
  166.2 4.7 %collective-permute-start.15 = (f32[64,1,130]{2,0,1:T(8,128)S(1)}, f32[64,1,130]{2,0,1:T(8,128)S(1)}, u32[]{:S(2)}, u32[]{:S(2)}) collective-permute-start(f32[64,1,130]{2,0,1:T(8,128)S(1)} %get-tuple-element.38), channel_id=1, source_target_pairs={{2,0},{0,2},{3,1},{1,3},{6,4},{4,6},{7,5},{5,7},{10,8},{8,10},{11,... | collective-permute-start | bytes 99848 | tf_op jit(solution)/shard_map/ppermute | solution.py:21
  167.7 4.3 %collective-permute-start.14 = (f32[64,1,130]{2,0,1:T(8,128)S(1)}, f32[64,1,130]{2,0,1:T(8,128)S(1)}, u32[]{:S(2)}, u32[]{:S(2)}) collective-permute-start(f32[64,1,130]{2,0,1:T(8,128)S(1)} %get-tuple-element.37), channel_id=1, source_target_pairs={{0,2},{2,0},{1,3},{3,1},{4,6},{6,4},{5,7},{7,5},{8,10},{10,8},{9,1... | collective-permute-start | bytes 99848 | tf_op jit(solution)/shard_map/ppermute | solution.py:19
  168.3 3.7 %copy-start.44 = (f32[64]{0:T(128)S(1)}, f32[64]{0:T(128)}, u32[]{:S(2)}) copy-start(f32[64]{0:T(128)} %get-tuple-element.74) | copy-start | bytes 772
  168.3 3.7 %copy-start.48 = (f32[64]{0:T(128)S(1)}, f32[64]{0:T(128)}, u32[]{:S(2)}) copy-start(f32[64]{0:T(128)} %get-tuple-element.75) | copy-start | bytes 772
  168.3 3.7 %copy-start.52 = (f32[64]{0:T(128)S(1)}, f32[64]{0:T(128)}, u32[]{:S(2)}) copy-start(f32[64]{0:T(128)} %get-tuple-element.76) | copy-start | bytes 772
  168.3 3.7 %copy-start.56 = (f32[64]{0:T(128)S(1)}, f32[64]{0:T(128)}, u32[]{:S(2)}) copy-start(f32[64]{0:T(128)} %get-tuple-element.77) | copy-start | bytes 772
  (33 other events, 25.3 us)
where the time goes:
time: 176 us; the launch traced here: 175 us
  starting transfers between devices  48.6 us (28%)
  local copies, waits for them, and re-layouts  44.4 us (25%)
  waiting for transfers between devices  34.2 us (19%)
  other arithmetic  31.5 us (18%)
  blocking collectives  13.7 us (8%)
    ppermute x16, starting transfers between devices, padded_2(): lax.ppermute(head, axis, [((i + 1) % count, i) for i in range(count)])  37.8 us
    ppermute x16, waiting for transfers between devices, padded_2(): lax.ppermute(tail, axis, [(i, (i + 1) % count) for i in range(count)])  21.7 us
    psum x4, blocking collectives, column_totals(): lax.psum(jnp.sum(atm_field, axis=0).astype(jnp.bfloat16), 'vert')  13.7 us
    slice x11, local copies, waits for them, and re-layouts, padded_2(): lax.slice_in_dim(cells, cells.shape[dim] - width, cells.shape[dim], axis=...  13 us
    ppermute x16, waiting for transfers between devices, padded_2(): lax.ppermute(head, axis, [((i + 1) % count, i) for i in range(count)])  12.6 us
    unnamed x133, local copies, waits for them, and re-layouts  11 us
    slice x8, other arithmetic, padded_2(): lax.slice_in_dim(cells, cells.shape[dim] - width, cells.shape[dim], axis=...  9.15 us
    ppermute x4, local copies, waits for them, and re-layouts, padded_2(): lax.ppermute(tail, axis, [(i, (i + 1) % count) for i in range(count)])  8.51 us
  transfers between devices with their start and end apart: 33, of which 8 were waited for; matrix products, arithmetic and copies ran while one was open for 35% of the time, Pallas kernels for 0%

commit v1 on v0

v1 whole, which is shorter than its diff:
```python
import functools

import jax
import jax.numpy as jnp
from jax import lax
from jax.experimental import pallas as pl
from jax.experimental.pallas import tpu as pltpu
from jax.sharding import PartitionSpec as P

F32 = jnp.float32
BF16 = jnp.bfloat16
W = 4
ZG = 16 * 8 + 16
G = 16


def rup(x, m):
    return (x + m - 1) // m * m


def lane_iota(rows):
    return lax.broadcasted_iota(jnp.int32, (rows, 128), 1)


def sub_iota(rows):
    return lax.broadcasted_iota(jnp.int32, (rows, 128), 0)


BT = 4


class Field:
    def __init__(self, levels, rows, total, z0, x0, c0, s0):
        self.L, self.R, self.total = levels, rows, total
        self.E = rows + 2 * W
        self.V = (levels + G - 1) // G
        self.full = levels // G
        self.tail = levels - self.full * G
        self.z0, self.x0, self.c0, self.s0 = z0, x0, c0, s0
        self.chunks = [(v, min(G, levels - v * G)) for v in range(self.V)]

    def groups(self, fn):
        if self.full:

            def step(v, carry):
                fn(v, G)
                return carry

            lax.fori_loop(0, self.full, step, 0)
        if self.tail:
            fn(self.full, self.tail)


def kernel(
    fa, fo, NR, H, C, flux_f, nba, entries,
    a_hbm, o_hbm, w_hbm, flux_ref, ac, oc, rl,
    ua_hbm, uo_hbm, ma_ref, mo_ref, rem_ref,
    a_own, o_own, a_ext, o_ext, a_w, a_e, o_w, o_e, a_cl, o_cl,
    a_sum, o_sum, wbuf,
    zs, zr, xf, xs, xr, cs, cr,
    a_vs, a_vr, o_vs, o_vr, a_us, a_ur, o_us, o_ur,
    sel, rs, rr,
    ld_sem, out_sem, z_ss, z_rs, x_ss, x_rs, c_ss, c_rs, v_ss, v_rs, r_ss, r_rs,
):
    def listed(p, e, i):
        return rl[i, p, e]

    hi = lax.axis_index("horiz")
    ci = lax.axis_index("comp")
    vi = lax.axis_index("vert")
    peers = H * C
    me = hi * C + ci
    west, east = lax.rem(hi + H - 1, H), lax.rem(hi + 1, H)
    north, south = lax.rem(ci + 1, C), lax.rem(ci + C - 1, C)
    other = 1 - vi
    MESH = pl.DeviceIdType.MESH

    loads = [
        pltpu.make_async_copy(a_hbm, a_own, ld_sem.at[0]),
        pltpu.make_async_copy(o_hbm, o_own, ld_sem.at[1]),
        pltpu.make_async_copy(w_hbm, wbuf, ld_sem.at[2]),
    ]
    for load in loads:
        load.start()

    barrier = pltpu.get_barrier_semaphore()

    def greet(k, carry):
        peer = lax.rem(me + k, peers)
        pl.semaphore_signal(
            barrier, inc=1, device_id={"horiz": peer // C, "comp": lax.rem(peer, C)}, device_id_type=MESH
        )
        return carry

    pl.semaphore_signal(barrier, inc=1, device_id={"vert": other}, device_id_type=MESH)
    lax.fori_loop(1, peers, greet, 0)

    def scalars(co, l):
        cx, cy, kd, km = co[0, l], co[1, l], co[2, l], co[3, l]
        return 1.0 - cx - cy - 4.0 * kd - km, cx + kd, cy + kd, kd, km

    lane1 = lane_iota(1)

    def spread(f, co, cl):
        def group(v, n):
            rows = [jnp.zeros((1, 128), F32) for _ in range(5)]
            for k in range(n):
                here = (lane1 // 8) == k
                rows = [jnp.where(here, s, r) for s, r in zip(scalars(co, v * G + k), rows)]
            for i in range(5):
                cl[v, i : i + 1, :] = rows[i]

        f.groups(group)

    spread(fa, ac, a_cl)
    spread(fo, oc, o_cl)

    def total_km(f, co):
        def add(l, s):
            return s + co[3, l]

        return lax.fori_loop(0, f.L, add, jnp.float32(0))

    a_k = total_km(fa, ac)
    o_k = total_km(fo, oc)

    sub8 = sub_iota(8)
    sub16 = sub_iota(16)

    def pack(f, own):
        lane = lane_iota(f.R)

        def group(v, n):
            acc = jnp.zeros((f.R, 128), F32)
            z_prev = None
            lost = jnp.zeros((16, 128), F32)
            for k in range(n):
                q = own[v * G + k]
                acc = jnp.where((lane // 8) == k, pltpu.roll(q, (8 * k + 4) % 128, 1), acc)
                z = jnp.where(sub8 < W, q[0:8], q[f.R - 8 : f.R])
                top = q[f.R - 1 : f.R]
                lost = jnp.where(sub16 == k, top - top.astype(BF16).astype(F32), lost)
                if k % 2 == 0:
                    z_prev = z
                else:
                    at = pl.multiple_of(f.z0 + v * ZG + (k - 1) * 8, 16)
                    zs[pl.ds(at, 16), :] = jnp.concatenate([z_prev, z], axis=0).astype(BF16)
            at = pl.multiple_of(f.z0 + v * ZG + n * 8, 16)
            zs[pl.ds(at, 16), :] = lost.astype(BF16)
            at = pl.multiple_of(f.x0 + v * f.R, 16)
            xf[pl.ds(at, f.R), :] = acc
            xs[pl.ds(at, f.R), :] = acc.astype(BF16)

        f.groups(group)
        for v in range(0, rup(f.V, 2), 2):
            parts = []
            for u in (v, v + 1):
                if u < f.V:
                    base = f.x0 + u * f.R
                    parts.append(
                        jnp.where(sub8 < W, xf[base : base + 8, :], xf[base + f.R - 8 : base + f.R, :])
                    )
                else:
                    parts.append(jnp.zeros((8, 128), F32))
            at = f.c0 + v * 8
            cs[at : at + 16, :] = jnp.concatenate(parts, axis=0).astype(BF16)

    row_nbrs = [north] if NR == 1 else [north, south]

    def slot_at(n):
        return n if NR == 1 else 1 - n

    def z_copy(f, n, i, base):
        v, cnt = f.chunks[i]
        at, size = f.z0 + v * ZG, cnt * 8 + 16
        return pltpu.make_async_remote_copy(
            src_ref=zs.at[pl.ds(at, size)],
            dst_ref=zr.at[slot_at(n), pl.ds(at, size)],
            send_sem=z_ss.at[n, base + i],
            recv_sem=z_rs.at[slot_at(n), base + i],
            device_id={"comp": row_nbrs[n]},
            device_id_type=MESH,
        )

    def x_copy(side):
        return pltpu.make_async_remote_copy(
            src_ref=xs,
            dst_ref=xr.at[1 - side],
            send_sem=x_ss.at[side],
            recv_sem=x_rs.at[1 - side],
            device_id={"horiz": west if side == 0 else east},
            device_id_type=MESH,
        )

    def c_copy(n, j):
        col = (west, hi, east)[j]
        return pltpu.make_async_remote_copy(
            src_ref=cs,
            dst_ref=cr.at[slot_at(n), 2 - j],
            send_sem=c_ss.at[n, j],
            recv_sem=c_rs.at[slot_at(n), 2 - j],
            device_id={"horiz": col, "comp": row_nbrs[n]},
            device_id_type=MESH,
        )

    oz = fa.V
    loads[0].wait()
    pack(fa, a_own)
    pl.semaphore_wait(barrier, peers)
    for i in range(fa.V):
        for n in range(NR):
            z_copy(fa, n, i, 0).start()
    loads[1].wait()
    pack(fo, o_own)
    for side in range(2):
        x_copy(side).start()
    for n in range(NR):
        for j in range(3):
            c_copy(n, j).start()
    for i in range(fo.V):
        for n in range(NR):
            z_copy(fo, n, i, oz).start()

    lane8 = lane_iota(8)

    def choose(p, carry):
        first, last = jnp.int32(0), jnp.int32(0)
        seen = jnp.int32(0)

        def look(e, st):
            first, last, seen = st
            s = listed(p, e, 0)
            here = (s // nba) == me
            b = lax.rem(s, nba)
            first = jnp.where(jnp.logical_and(here, seen == 0), b, first)
            last = jnp.where(here, b, last)
            seen = jnp.where(here, 1, seen)
            return first, last, seen

        if entries <= 16:
            st = (first, last, seen)
            for e in range(entries):
                st = look(e, st)
        else:
            st = lax.fori_loop(0, entries, look, (first, last, seen))
        first, last, _ = st
        want = jnp.where(sub8 < flux_f, first, last) + lax.rem(sub8, flux_f) * nba
        at = pl.multiple_of(p * 8, 8)
        sel[pl.ds(at, 8), :] = jnp.where(lane8 == want, 1.0, 0.0)
        return carry

    lax.fori_loop(0, peers, choose, 0)
    depth = flux_f * nba
    picked = jnp.dot(
        sel[:, 0:depth].astype(BF16),
        flux_ref[...].reshape(depth, 128),
        preferred_element_type=F32,
    )
    rs[...] = picked.reshape(peers, 8, 128)
    rr[me] = rs[me]

    def r_copy(k):
        peer = lax.rem(me + k, peers)
        return pltpu.make_async_remote_copy(
            src_ref=rs.at[peer],
            dst_ref=rr.at[me],
            send_sem=r_ss.at[k],
            recv_sem=r_rs.at[k],
            device_id={"horiz": peer // C, "comp": lax.rem(peer, C)},
            device_id_type=MESH,
        )

    def r_start(k, carry):
        r_copy(k).start()
        return carry

    lax.fori_loop(1, peers, r_start, 0)

    def stencil(E, q, wv, ev, a, b, c, d):
        return a * q + b * wv + c * pltpu.roll(q, 1, 0) + d * (ev + pltpu.roll(q, E - 1, 0))

    def one_pass(f, co, cl, own, ext, wt, et, sums, mean, first=False, last=False, after=None):
        E, R = f.E, f.R
        lane = lane_iota(E)
        low = lax.rem(lane, 8) < W
        is0, is127 = lane == 0, lane == 127
        oz_f = 0 if f is fa else fa.V
        nsum = 6 if first else 3
        if not last:
            sums[...] = jnp.zeros_like(sums)

        def rows_of(ref, idx, at):
            t = ref[idx + (pl.ds(pl.multiple_of(at - lax.rem(at, 16), 16), 16), slice(None))].astype(F32)
            return t

        def group(v, n):
            cc = [cl[v, i : i + 1, :] for i in range(5)]
            if first:
                for m in range(NR):
                    size = n * 8 + 16
                    at = f.z0 + v * ZG
                    at = at if isinstance(at, int) else pl.multiple_of(at, 16)
                    pltpu.make_async_remote_copy(
                        src_ref=zs.at[pl.ds(at, size)],
                        dst_ref=zr.at[m, pl.ds(at, size)],
                        send_sem=z_ss.at[m, oz_f + v],
                        recv_sem=z_rs.at[m, oz_f + v],
                        device_id={"comp": row_nbrs[m]},
                        device_id_type=MESH,
                    ).wait_recv()
                xat = f.x0 + v * R
                xat = xat if isinstance(xat, int) else pl.multiple_of(xat, 16)
                mine = xf[pl.ds(xat, R), :]
                xw = xr[0, pl.ds(xat, R), :].astype(F32)
                xe = xr[1, pl.ds(xat, R), :].astype(F32)
                pair = pl.multiple_of(f.c0 + (v // 2) * 16, 16)
                odd = lax.rem(v, 2) == 1

                def corner(j):
                    ts = [cr[m, j, pl.ds(pair, 16), :].astype(F32) for m in range(NR)]
                    hs = [jnp.where(odd, t[8:16], t[0:8]) for t in ts]
                    return hs[0] if NR == 1 else jnp.where(sub8 < W, hs[0], hs[1])

                mine = jnp.concatenate([mine, corner(1)], axis=0)
                xw = jnp.concatenate([xw, corner(0)], axis=0)
                xe = jnp.concatenate([xe, corner(2)], axis=0)
                qw = jnp.where(low, xw, mine)
                qe = jnp.where(low, mine, xe)
                sums[4] += qw
                sums[5] += qe
            else:
                qw = wt[v] + cc[4] * mean[1]
                qe = et[v] + cc[4] * mean[2]
            p = jnp.where(lax.rem(lane, 8) == W - 1, qw, pltpu.roll(qe, 126, 1))
            if not last:
                uw = stencil(E, qw, pltpu.roll(qw, 1, 1), pltpu.roll(qw, 127, 1), *cc[:4])
                ue = stencil(E, qe, pltpu.roll(qe, 1, 1), pltpu.roll(qe, 127, 1), *cc[:4])
                wt[v] = uw
                et[v] = ue
                sums[1] += uw
                sums[2] += ue
            total = sums[0] if not last else None
            total0 = sums[3] if first else None
            if first:
                at = pl.multiple_of(f.z0 + v * ZG + n * 8, 16)
                lost = zr[NR - 1, pl.ds(at, 16), :].astype(F32)
            for k0 in range(0, n, BT):
                batch = range(k0, k0 + BT)
                qs = []
                for k in batch:
                    l = v * G + k
                    if first:
                        if k % 2 == 0:
                            at = pl.multiple_of(f.z0 + v * ZG + k * 8, 16)
                            ts = [zr[m, pl.ds(at, 16), :].astype(F32) for m in range(NR)]
                            zpair = ts[0] if NR == 1 else jnp.where(lax.rem(sub_iota(16), 8) < W, ts[0], ts[1])
                        edge = zpair[(k % 2) * 8 : (k % 2) * 8 + 8]
                        edge = edge + jnp.where(sub8 == 7, lost[k : k + 1], 0.0)
                        q = jnp.concatenate([own[l], edge], axis=0)
                        total0 = total0 + q
                    else:
                        q = ext[l] + co[3, l] * mean[0]
                    qs.append(q)
                us = []
                for k, q in zip(batch, qs):
                    a, b, c, d, km = scalars(co, v * G + k)
                    h = pltpu.roll(p, (125 - 8 * k) % 128, 1)
                    wv = jnp.where(is0, h, pltpu.roll(q, 1, 1))
                    ev = jnp.where(is127, h, pltpu.roll(q, 127, 1))
                    us.append(stencil(E, q, wv, ev, a, b, c, d))
                for k, u in zip(batch, us):
                    l = v * G + k
                    if last:
                        own[l] = u[0:R]
                    else:
                        ext[l] = u
                        total = total + u
            if not last:
                sums[0] = total
            if first:
                sums[3] = total0
            if after is not None:
                after(v, n)

        f.groups(group)

    def fold(x):
        for s in (8, 16, 32, 64):
            x = x + pltpu.roll(x, s, 1)
        return x

    def v_copy(src, dst, i):
        return pltpu.make_async_remote_copy(
            src_ref=src, dst_ref=dst, send_sem=v_ss.at[i], recv_sem=v_rs.at[i],
            device_id={"vert": other}, device_id_type=MESH,
        )

    def send0(f, sums, kk, vs, vr, i):
        for j in range(6):
            s = sums[j]
            vs[j, 0 : f.E, :] = s if j in (0, 3) else fold(s)
        vs[6, 0:8, :] = jnp.full((8, 128), kk, F32)
        cp = v_copy(vs, vr, i)
        cp.start()
        return cp

    def send1(f, sums, us, ur, slot, i):
        for j in range(3 if slot == 0 else 1):
            us[slot, j] = sums[j] if j == 0 else fold(sums[j])
        if slot == 1:
            cp = v_copy(us.at[slot, 0], ur.at[slot, 0], i)
        else:
            cp = v_copy(us.at[slot], ur.at[slot], i)
        cp.start()
        return cp

    def means0(f, vs, vr):
        inv = F32(1.0 / f.total)
        ksum = (vs[6, 0:1, :] + vr[6, 0:1, :]) * inv
        m0 = [(vs[3 + j] + vr[3 + j]) * inv for j in range(3)]
        m1 = [(vs[j] + vr[j]) * inv + ksum * m0[j] for j in range(3)]
        return m0, m1, ksum

    for side in range(2):
        x_copy(1 - side).wait_recv()
    for n in range(NR):
        for j in range(3):
            c_copy(n, j).wait_recv()

    one_pass(fa, ac, a_cl, a_own, a_ext, a_w, a_e, a_sum, None, first=True)
    a0 = send0(fa, a_sum, a_k, a_vs, a_vr, 0)
    one_pass(fo, oc, o_cl, o_own, o_ext, o_w, o_e, o_sum, None, first=True)
    o0 = send0(fo, o_sum, o_k, o_vs, o_vr, 1)

    def r_wait(k, carry):
        r_copy(k).wait_recv()
        return carry

    lax.fori_loop(1, peers, r_wait, 0)
    loads[2].wait()
    nbo = rem_ref.shape[1]
    subo = sub_iota(nbo)

    def entry(e, acc):
        s = listed(me, e, 0)
        dev = s // nba
        t = lax.rem(listed(me, e, 1), nbo)
        wi = listed(me, e, 2)

        def before(x, got):
            return jnp.where(listed(me, x, 0) // nba == dev, jnp.int32(1), got)

        second = jnp.int32(0)
        if isinstance(e, int):
            for x in range(e):
                second = before(x, second)
        else:
            second = lax.fori_loop(0, e, before, second)
        prod = jnp.dot(rr[dev].astype(BF16), wbuf[wi], preferred_element_type=F32)
        hit = subo == t
        out = []
        for f in range(flux_f):
            row = jnp.where(second == 1, prod[flux_f + f : flux_f + f + 1], prod[f : f + 1])
            out.append(acc[f] + jnp.where(hit, row, 0.0))
        return tuple(out)

    acc = tuple(jnp.zeros((nbo, 128), F32) for _ in range(flux_f))
    if entries <= 16:
        for e in range(entries):
            acc = entry(e, acc)
    else:
        acc = lax.fori_loop(0, entries, entry, acc)
    for f in range(flux_f):
        rem_ref[f] = acc[f]

    def keep(f, sums, ms):
        for j in range(3):
            sums[j] = ms[j]

    a0.wait()
    am0, am1, a_ks = means0(fa, a_vs, a_vr)
    for j in range(3):
        a_vs[j] = am0[j]
        a_vs[3 + j] = am1[j]
    one_pass(fa, ac, a_cl, a_own, a_ext, a_w, a_e, a_sum, a_vs.at[0:3])
    a1 = send1(fa, a_sum, a_us, a_ur, 0, 2)

    o0.wait()
    om0, om1, o_ks = means0(fo, o_vs, o_vr)
    for j in range(3):
        o_vs[j] = om0[j]
        o_vs[3 + j] = om1[j]
    one_pass(fo, oc, o_cl, o_own, o_ext, o_w, o_e, o_sum, o_vs.at[0:3])
    o1 = send1(fo, o_sum, o_us, o_ur, 0, 3)

    one_pass(fa, ac, a_cl, a_own, a_ext, a_w, a_e, a_sum, a_vs.at[3:6])
    a2 = send1(fa, a_sum, a_us, a_ur, 1, 4)
    one_pass(fo, oc, o_cl, o_own, o_ext, o_w, o_e, o_sum, o_vs.at[3:6])
    o2 = send1(fo, o_sum, o_us, o_ur, 1, 5)

    def mean2(f, us, ur, vs, ks):
        inv = F32(1.0 / f.total)
        for j in range(3):
            vs[j] = (us[0, j] + ur[0, j]) * inv + ks * vs[3 + j]

    def out_copies(own, hbm, base):
        def after(v, n):
            at = v * G
            pltpu.make_async_copy(own.at[pl.ds(at, n)], hbm.at[pl.ds(at, n)], out_sem.at[base + v]).start()

        return after

    a1.wait()
    mean2(fa, a_us, a_ur, a_vs, a_ks)
    one_pass(fa, ac, a_cl, a_own, a_ext, a_w, a_e, a_sum, a_vs.at[0:3], last=True, after=out_copies(a_own, ua_hbm, 0))
    o1.wait()
    mean2(fo, o_us, o_ur, o_vs, o_ks)
    one_pass(fo, oc, o_cl, o_own, o_ext, o_w, o_e, o_sum, o_vs.at[0:3], last=True, after=out_copies(o_own, uo_hbm, fa.V))
    a2.wait()
    o2.wait()
    ma_ref[...] = ((a_us[1, 0] + a_ur[1, 0]) * F32(1.0 / fa.total) + a_ks * a_vs[0])[0 : fa.R]
    mo_ref[...] = ((o_us[1, 0] + o_ur[1, 0]) * F32(1.0 / fo.total) + o_ks * o_vs[0])[0 : fo.R]

    for f, own, hbm, base in ((fa, a_own, ua_hbm, 0), (fo, o_own, uo_hbm, fa.V)):
        for v, n in f.chunks:
            at = v * G
            pltpu.make_async_copy(own.at[pl.ds(at, n)], hbm.at[pl.ds(at, n)], out_sem.at[base + v]).wait()
    for side in range(2):
        x_copy(side).wait_send()
    for n in range(NR):
        for j in range(3):
            c_copy(n, j).wait_send()
        for i in range(fa.V):
            z_copy(fa, n, i, 0).wait_send()
        for i in range(fo.V):
            z_copy(fo, n, i, oz).wait_send()

    def r_done(k, carry):
        r_copy(k).wait_send()
        return carry

    lax.fori_loop(1, peers, r_done, 0)


def body(H, C, KV, atm_state, atm_coeffs, ocean_state, ocean_coeffs, atm_flux, remap_weights, remap_list, ocean_mask):
    la, ra, _ = atm_state.shape
    lo, ro, _ = ocean_state.shape
    flux_f, nba, _ = atm_flux.shape
    entries = remap_list.shape[1]
    nbo = ocean_mask.shape[0]
    peers = H * C
    NR = 1 if C == 2 else 2
    remap_list = jnp.transpose(remap_list, (2, 0, 1))
    va, vo = (la + G - 1) // G, (lo + G - 1) // G
    fa = Field(la, ra, KV * la, 0, 0, 0, 0)
    fo = Field(lo, ro, KV * lo, va * ZG, va * ra, rup(va, 2) * 8, 0)
    zrows = (va + vo) * ZG
    xrows = va * ra + vo * ro
    crows = (rup(va, 2) + rup(vo, 2)) * 8
    V = pltpu.VMEM
    DMA = pltpu.SemaphoreType.DMA
    scratch = [
        V((la, ra, 128), F32), V((lo, ro, 128), F32),
        V((la, fa.E, 128), F32), V((lo, fo.E, 128), F32),
        V((va, fa.E, 128), F32), V((va, fa.E, 128), F32),
        V((vo, fo.E, 128), F32), V((vo, fo.E, 128), F32),
        V((va, 8, 128), F32), V((vo, 8, 128), F32),
        V((6, fa.E, 128), F32), V((6, fo.E, 128), F32),
        V(remap_weights.shape, BF16),
        V((zrows, 128), BF16), V((NR, zrows, 128), BF16),
        V((xrows, 128), F32), V((xrows, 128), BF16), V((2, xrows, 128), BF16),
        V((crows, 128), BF16), V((NR, 3, crows, 128), BF16),
        V((7, fa.E, 128), F32), V((7, fa.E, 128), F32),
        V((7, fo.E, 128), F32), V((7, fo.E, 128), F32),
        V((2, 3, fa.E, 128), F32), V((2, 3, fa.E, 128), F32),
        V((2, 3, fo.E, 128), F32), V((2, 3, fo.E, 128), F32),
        V((peers * 8, 128), F32), V((peers, 8, 128), F32), V((peers, 8, 128), F32),
        DMA((3,)), DMA((va + vo,)),
        DMA((NR, va + vo)), DMA((NR, va + vo)),
        DMA((2,)), DMA((2,)),
        DMA((NR, 3)), DMA((NR, 3)),
        DMA((6,)), DMA((6,)),
        DMA((peers,)), DMA((peers,)),
    ]
    anyspec = pl.BlockSpec(memory_space=pl.ANY)
    hbm = pl.BlockSpec(memory_space=pltpu.HBM)
    vspec = pl.BlockSpec(memory_space=pltpu.VMEM)
    sspec = pl.BlockSpec(memory_space=pltpu.SMEM)
    ua, uo, ma, mo, rem = pl.pallas_call(
        functools.partial(kernel, fa, fo, NR, H, C, flux_f, nba, entries),
        out_shape=(
            jax.ShapeDtypeStruct((la, ra, 128), F32),
            jax.ShapeDtypeStruct((lo, ro, 128), F32),
            jax.ShapeDtypeStruct((ra, 128), F32),
            jax.ShapeDtypeStruct((ro, 128), F32),
            jax.ShapeDtypeStruct((flux_f, nbo, 128), F32),
        ),
        in_specs=[hbm, hbm, hbm, vspec, sspec, sspec, sspec],
        out_specs=(anyspec, anyspec, vspec, vspec, vspec),
        scratch_shapes=scratch,
        compiler_params=pltpu.CompilerParams(
            collective_id=0, has_side_effects=True, vmem_limit_bytes=32 * 1024 * 1024
        ),
    )(*[pltpu.with_memory_space_constraint(x, pltpu.HBM) for x in (atm_state, ocean_state, remap_weights)], atm_flux, atm_coeffs, ocean_coeffs, remap_list)
    return (
        ua + atm_coeffs[3][:, None, None] * ma[None],
        uo + ocean_coeffs[3][:, None, None] * mo[None],
        rem * ocean_mask.astype(F32)[None],
    )


def solution(mesh):
    H, C, KV = mesh.shape["horiz"], mesh.shape["comp"], mesh.shape["vert"]
    return jax.shard_map(
        functools.partial(body, H, C, KV),
        mesh=mesh,
        in_specs=(
            P("vert", ("runs", "comp"), "horiz"),
            P(None, "vert"),
            P("vert", ("runs", "comp"), "horiz"),
            P(None, "vert"),
            P("vert", ("runs", "horiz", "comp"), None),
            P(),
            P(),
            P(("horiz", "comp"), None),
        ),
        out_specs=(
            P("vert", ("runs", "comp"), "horiz"),
            P("vert", ("runs", "comp"), "horiz"),
            P("vert", ("runs", "horiz", "comp"), None),
        ),
        check_vma=False,
    )
```

time: 176 us -> 30.5 us (0.17)
  starting transfers between devices: 48.6 us -> 0 us
  local copies, waits for them, and re-layouts: 44.4 us -> 2.79 us
  waiting for transfers between devices: 34.2 us -> 0 us
  other arithmetic: 31.5 us -> 2.57 us
  Pallas kernels: 0 us -> 24.1 us
  blocking collectives: 13.7 us -> 0 us
    ppermute x32 -> x0, starting transfers between devices: 42.6 us -> none  [the longest x16 37.8 us: padded_2(): lax.ppermute(head, axis, [((i + 1) % count, i) for i in range(count)])]
    ppermute x32 -> x0, waiting for transfers between devices: 34.2 us -> none  [the longest x16 21.7 us: padded_2(): lax.ppermute(tail, axis, [(i, (i + 1) % count) for i in range(count)])]
    pallas_call x0 -> x1, Pallas kernels: none -> 24.1 us  [body(): pl.pallas_call(functools.partial(kernel, fa, fo, NR, H, C, flux_f, nba, e...]
    slice x14 -> x0, local copies, waits for them, and re-layouts: 16.6 us -> none  [the longest x11 13 us: padded_2(): lax.slice_in_dim(cells, cells.shape[dim] - width, cells.shape[dim], axis=...]
    reduce_sum x9 -> x0, other arithmetic: 14.9 us -> none  [the longest x4 7.69 us: column_totals(): jnp.sum(ocean_field, axis=0).astype(jnp.bfloat16)]
    psum x4 -> x0, blocking collectives: 13.7 us -> none  [column_totals(): lax.psum(jnp.sum(atm_field, axis=0).astype(jnp.bfloat16), 'vert')]
    ppermute x8 -> x0, local copies, waits for them, and re-layouts: 12.9 us -> none  [the longest x4 8.51 us: padded_2(): lax.ppermute(tail, axis, [(i, (i + 1) % count) for i in range(count)])]
    slice x8 -> x0, other arithmetic: 9.15 us -> none  [padded_2(): lax.slice_in_dim(cells, cells.shape[dim] - width, cells.shape[dim], axis=...]
  transfers between devices with their start and end apart: 33 -> 0, of which waited for: 8 -> 0; matrix products, arithmetic and copies ran while one was open for 35% -> 0% of each run, Pallas kernels for 0% -> 0%
where the time goes in v1:
time: 30.5 us; the launch traced here: 30.1 us
  Pallas kernels  24.1 us (79%)
  local copies, waits for them, and re-layouts  2.79 us (9%)
  other arithmetic  2.57 us (8%)
  between operations  0.66 us (2%)
    pallas_call x1, Pallas kernels, body(): pl.pallas_call(functools.partial(kernel, fa, fo, NR, H, C, flux_f, nba, e...  24.1 us
    unnamed x10, local copies, waits for them, and re-layouts  2.78 us
    add x1, other arithmetic, body(): ua + atm_coeffs[3][:, None, None] * ma[None]  1.12 us
    add x1, other arithmetic, body(): uo + ocean_coeffs[3][:, None, None] * mo[None]  0.84 us
    mul x1, other arithmetic, body(): rem * ocean_mask.astype(F32)[None]  0.61 us

profile of v1, /device:TPU:0, one launch (start us, length us, event | category | flops | bytes accessed | tf_op | source)
XLA Modules:
  0.0 30.1 jit_solution(9621389582321468510)
XLA Ops:
  0.6 0.0 copy-start
  0.6 0.7 %copy-done = bf16[4,16,128]{2,1,0:T(8,128)(2,1)S(1)} copy-done((bf16[4,16,128]{2,1,0:T(8,128)(2,1)S(1)}, bf16[4,16,128]{2,1,0:T(8,128)(2,1)}, u32[]{:S(2)}) %copy-start) | copy-done | bytes 16408
  1.4 0.0 copy-start.1
  1.4 0.7 %copy-done.1 = s32[8,8,3]{1,0,2:T(8,128)S(1)} copy-done((s32[8,8,3]{1,0,2:T(8,128)S(1)}, s32[8,8,3]{1,0,2:T(8,128)}, u32[]{:S(2)}) %copy-start.1) | copy-done | bytes 792
  2.1 0.0 copy-start.2
  2.1 0.7 %copy-done.2 = f32[4,40]{1,0:T(4,128)S(1)} copy-done((f32[4,40]{1,0:T(4,128)S(1)}, f32[4,40]{1,0:T(4,128)}, u32[]{:S(2)}) %copy-start.2) | copy-done | bytes 664
  2.7 0.0 copy-start.3
  2.7 0.7 %copy-done.3 = f32[4,64]{1,0:T(4,128)S(1)} copy-done((f32[4,64]{1,0:T(4,128)S(1)}, f32[4,64]{1,0:T(4,128)}, u32[]{:S(2)}) %copy-start.3) | copy-done | bytes 1048
  3.4 24.1 %shard_map.103 = (f32[64,32,128]{2,1,0:T(8,128)S(1)}, f32[40,16,128]{2,1,0:T(8,128)S(1)}, f32[32,128]{1,0:T(8,128)S(1)}, f32[16,128]{1,0:T(8,128)S(1)}, f32[4,8,128]{2,1,0:T(8,128)S(1)}) custom-call(f32[64,32,128]{2,1,0:T(8,128)} %a_hbm.1, f32[40,16,128]{2,1,0:T(8,128)} %o_hbm.1, bf16[32,128,128]{2,1,0:T(8,128)(2,1)} %w_hbm.1, ...), custom_call_target="tpu_custom_call" | custom-call | tf_op jit(solution)/shard_map/pallas_call | solution.py:589
  27.5 0.8 %multiply_add_fusion.1 = f32[40,16,128]{2,1,0:T(8,128)} fusion(f32[40,16,128]{2,1,0:T(8,128)S(1)} %get-tuple-element.10, f32[16,128]{1,0:T(8,128)S(1)} %get-tuple-element.11, f32[40]{0:T(128)S(1)} %slice_bitcast_fusion), kind=kLoop, calls=%fused_computation.1 | loop fusion | flops 163840 | bytes 663712 | tf_op jit(solution)/shard_map/add | solution.py:607
  28.3 0.0 copy-start.4
  28.3 1.1 %multiply_add_fusion = f32[64,32,128]{2,1,0:T(8,128)} fusion(f32[64,32,128]{2,1,0:T(8,128)S(1)} %get-tuple-element.8, f32[32,128]{1,0:T(8,128)S(1)} %get-tuple-element.9, f32[64]{0:T(128)S(1)} %slice_bitcast_fusion.1), kind=kLoop, calls=%fused_computation | loop fusion | flops 524288 | bytes 2113792 | tf_op jit(solution)/shard_map/add | solution.py:606
  29.5 0.0 copy-done.4
  29.5 0.6 %broadcast_multiply_fusion = f32[4,8,128]{2,1,0:T(8,128)} fusion(f32[4,8,128]{2,1,0:T(8,128)S(1)} %get-tuple-element.12, f32[8,128]{1,0:T(8,128)S(1)} %convert_element_type.3), kind=kLoop, calls=%fused_computation.2 | loop fusion | flops 4096 | bytes 36864 | tf_op jit(solution)/shard_map/mul | solution.py:608
  (3 shorter events, 0.0 us)
Async XLA Ops:
  0.6 0.7 %copy-start = (bf16[4,16,128]{2,1,0:T(8,128)(2,1)S(1)}, bf16[4,16,128]{2,1,0:T(8,128)(2,1)}, u32[]{:S(2)}) copy-start(bf16[4,16,128]{2,1,0:T(8,128)(2,1)} %flux_ref.1) | copy-start | bytes 49156
  1.4 0.7 %copy-start.1 = (s32[8,8,3]{1,0,2:T(8,128)S(1)}, s32[8,8,3]{1,0,2:T(8,128)}, u32[]{:S(2)}) copy-start(s32[8,8,3]{1,0,2:T(8,128)} %param.14) | copy-start | bytes 2308
  2.1 0.7 %copy-start.2 = (f32[4,40]{1,0:T(4,128)S(1)}, f32[4,40]{1,0:T(4,128)}, u32[]{:S(2)}) copy-start(f32[4,40]{1,0:T(4,128)} %oc.1) | copy-start | bytes 1924
  2.7 0.7 %copy-start.3 = (f32[4,64]{1,0:T(4,128)S(1)}, f32[4,64]{1,0:T(4,128)}, u32[]{:S(2)}) copy-start(f32[4,64]{1,0:T(4,128)} %ac.1) | copy-start | bytes 3076
  28.3 1.1 %copy-start.4 = (s32[8,128]{1,0:T(8,128)S(1)}, s32[8,128]{1,0:T(8,128)}, u32[]{:S(2)}) copy-start(s32[8,128]{1,0:T(8,128)} %param.15) | copy-start | bytes 12292

commit v2 on v1

--- a/solution.py
+++ b/solution.py
@@ -54,7 +54,7 @@
 def kernel(
     fa, fo, NR, H, C, flux_f, nba, entries,
     a_hbm, o_hbm, w_hbm, flux_ref, ac, oc, rl,
-    ua_hbm, uo_hbm, ma_ref, mo_ref, rem_ref,
+    ua_hbm, uo_hbm, ma_ref, mo_ref, rem_ref, ka_ref, ko_ref,
     a_own, o_own, a_ext, o_ext, a_w, a_e, o_w, o_e, a_cl, o_cl,
     a_sum, o_sum, wbuf,
     zs, zr, xf, xs, xr, cs, cr,
@@ -115,14 +115,15 @@
     spread(fa, ac, a_cl)
     spread(fo, oc, o_cl)
 
-    def total_km(f, co):
+    def total_km(f, co, kept):
         def add(l, s):
+            kept[0, l] = co[3, l]
             return s + co[3, l]
 
         return lax.fori_loop(0, f.L, add, jnp.float32(0))
 
-    a_k = total_km(fa, ac)
-    o_k = total_km(fo, oc)
+    a_k = total_km(fa, ac, ka_ref)
+    o_k = total_km(fo, oc, ko_ref)
 
     sub8 = sub_iota(8)
     sub16 = sub_iota(16)
@@ -586,7 +587,7 @@
     hbm = pl.BlockSpec(memory_space=pltpu.HBM)
     vspec = pl.BlockSpec(memory_space=pltpu.VMEM)
     sspec = pl.BlockSpec(memory_space=pltpu.SMEM)
-    ua, uo, ma, mo, rem = pl.pallas_call(
+    ua, uo, ma, mo, rem, ka, ko = pl.pallas_call(
         functools.partial(kernel, fa, fo, NR, H, C, flux_f, nba, entries),
         out_shape=(
             jax.ShapeDtypeStruct((la, ra, 128), F32),
@@ -594,17 +595,26 @@
             jax.ShapeDtypeStruct((ra, 128), F32),
             jax.ShapeDtypeStruct((ro, 128), F32),
             jax.ShapeDtypeStruct((flux_f, nbo, 128), F32),
+            jax.ShapeDtypeStruct((1, la), F32),
+            jax.ShapeDtypeStruct((1, lo), F32),
         ),
         in_specs=[hbm, hbm, hbm, vspec, sspec, sspec, sspec],
-        out_specs=(anyspec, anyspec, vspec, vspec, vspec),
+        out_specs=(anyspec, anyspec, vspec, vspec, vspec, sspec, sspec),
         scratch_shapes=scratch,
         compiler_params=pltpu.CompilerParams(
             collective_id=0, has_side_effects=True, vmem_limit_bytes=32 * 1024 * 1024
         ),
-    )(*[pltpu.with_memory_space_constraint(x, pltpu.HBM) for x in (atm_state, ocean_state, remap_weights)], atm_flux, atm_coeffs, ocean_coeffs, remap_list)
+    )(
+        *[
+            pltpu.with_memory_space_constraint(x, pltpu.HBM)
+            for x in (
+                atm_state, ocean_state, remap_weights, atm_flux, atm_coeffs, ocean_coeffs, remap_list
+            )
+        ]
+    )
     return (
-        ua + atm_coeffs[3][:, None, None] * ma[None],
-        uo + ocean_coeffs[3][:, None, None] * mo[None],
+        ua + ka[0][:, None, None] * ma[None],
+        uo + ko[0][:, None, None] * mo[None],
         rem * ocean_mask.astype(F32)[None],
     )
 

time: 30.5 us -> 28.4 us (0.931)
  local copies, waits for them, and re-layouts: 2.79 us -> 0.01 us
  Pallas kernels: 24.1 us -> 25 us
    unnamed x10 -> x2, local copies, waits for them, and re-layouts: 2.78 us -> 0.01 us
    pallas_call x1, Pallas kernels: 24.1 us -> 25 us  [body(): pl.pallas_call(functools.partial(kernel, fa, fo, NR, H, C, flux_f, nba, e...]
where the time goes in v2:
time: 28.4 us; the launch traced here: 28.2 us
  Pallas kernels  25 us (88%)
  other arithmetic  2.57 us (9%)
  between operations  0.64 us (2%)
    pallas_call x1, Pallas kernels, body(): pl.pallas_call(functools.partial(kernel, fa, fo, NR, H, C, flux_f, nba, e...  25 us
    add x1, other arithmetic, body(): ua + ka[0][:, None, None] * ma[None]  1.12 us
    add x1, other arithmetic, body(): uo + ko[0][:, None, None] * mo[None]  0.84 us
    mul x1, other arithmetic, body(): rem * ocean_mask.astype(F32)[None]  0.61 us

profile of v2, /device:TPU:0, one launch (start us, length us, event | category | flops | bytes accessed | tf_op | source)
XLA Modules:
  0.0 28.2 jit_solution(7343799630507065954)
XLA Ops:
  0.6 25.0 %shard_map.103 = (f32[64,32,128]{2,1,0:T(8,128)S(1)}, f32[40,16,128]{2,1,0:T(8,128)S(1)}, f32[32,128]{1,0:T(8,128)S(1)}, f32[16,128]{1,0:T(8,128)S(1)}, f32[4,8,...) custom-call(f32[64,32,128]{2,1,0:T(8,128)} %a_hbm.1, f32[40,16,128]{2,1,0:T(8,128)} %o_hbm.1, ...), custom_call_target="tpu_custom_call" | custom-call | tf_op jit(solution)/shard_map/pallas_call | solution.py:590
  25.6 0.8 %multiply_add_fusion.1 = f32[40,16,128]{2,1,0:T(8,128)} fusion(f32[40,16,128]{2,1,0:T(8,128)S(1)} %get-tuple-element.13, f32[16,128]{1,0:T(8,128)S(1)} %get-tuple-element.15, f32[40]{0:T(128)S(1)} %bitcast.4), kind=kLoop, calls=%fused_computation.1 | loop fusion | flops 163840 | bytes 663712 | tf_op jit(solution)/shard_map/add | solution.py:617
  26.4 0.0 copy-start
  26.4 1.1 %multiply_add_fusion = f32[64,32,128]{2,1,0:T(8,128)} fusion(f32[64,32,128]{2,1,0:T(8,128)S(1)} %get-tuple-element.10, f32[32,128]{1,0:T(8,128)S(1)} %get-tuple-element.12, f32[64]{0:T(128)S(1)} %bitcast.3), kind=kLoop, calls=%fused_computation | loop fusion | flops 524288 | bytes 2113792 | tf_op jit(solution)/shard_map/add | solution.py:616
  27.6 0.0 copy-done
  27.6 0.6 %broadcast_multiply_fusion = f32[4,8,128]{2,1,0:T(8,128)} fusion(f32[4,8,128]{2,1,0:T(8,128)S(1)} %get-tuple-element.16, f32[8,128]{1,0:T(8,128)S(1)} %convert_element_type.3), kind=kLoop, calls=%fused_computation.2 | loop fusion | flops 4096 | bytes 36864 | tf_op jit(solution)/shard_map/mul | solution.py:618
  (1 shorter events, 0.0 us)
Async XLA Ops:
  26.4 1.1 %copy-start = (s32[8,128]{1,0:T(8,128)S(1)}, s32[8,128]{1,0:T(8,128)}, u32[]{:S(2)}) copy-start(s32[8,128]{1,0:T(8,128)} %param.15) | copy-start | bytes 12292

commit v3 on v2

--- a/solution.py
+++ b/solution.py
@@ -26,7 +26,7 @@
     return lax.broadcasted_iota(jnp.int32, (rows, 128), 0)
 
 
-BT = 4
+BT = 8
 
 
 class Field:
@@ -207,17 +207,17 @@
     oz = fa.V
     loads[0].wait()
     pack(fa, a_own)
-    pl.semaphore_wait(barrier, peers)
-    for i in range(fa.V):
-        for n in range(NR):
-            z_copy(fa, n, i, 0).start()
     loads[1].wait()
     pack(fo, o_own)
+    pl.semaphore_wait(barrier, peers)
     for side in range(2):
         x_copy(side).start()
     for n in range(NR):
         for j in range(3):
             c_copy(n, j).start()
+    for i in range(fa.V):
+        for n in range(NR):
+            z_copy(fa, n, i, 0).start()
     for i in range(fo.V):
         for n in range(NR):
             z_copy(fo, n, i, oz).start()

time: 28.4 us -> 28.3 us (level)
  no operation moved by 1% of the time
where the time goes in v3:
time: 28.3 us; the launch traced here: 28.1 us
  Pallas kernels  24.9 us (88%)
  other arithmetic  2.57 us (9%)
  between operations  0.64 us (2%)
    pallas_call x1, Pallas kernels, body(): pl.pallas_call(functools.partial(kernel, fa, fo, NR, H, C, flux_f, nba, e...  24.9 us
    add x1, other arithmetic, body(): ua + ka[0][:, None, None] * ma[None]  1.12 us
    add x1, other arithmetic, body(): uo + ko[0][:, None, None] * mo[None]  0.84 us
    mul x1, other arithmetic, body(): rem * ocean_mask.astype(F32)[None]  0.61 us

profile of v3, /device:TPU:0, one launch (start us, length us, event | category | flops | bytes accessed | tf_op | source)
XLA Modules:
  0.0 28.1 jit_solution(13548087921632768869)
XLA Ops:
  0.6 24.9 %shard_map.103 = (f32[64,32,128]{2,1,0:T(8,128)S(1)}, f32[40,16,128]{2,1,0:T(8,128)S(1)}, f32[32,128]{1,0:T(8,128)S(1)}, f32[16,128]{1,0:T(8,128)S(1)}, f32[4,8,...) custom-call(f32[64,32,128]{2,1,0:T(8,128)} %a_hbm.1, f32[40,16,128]{2,1,0:T(8,128)} %o_hbm.1, ...), custom_call_target="tpu_custom_call" | custom-call | tf_op jit(solution)/shard_map/pallas_call | solution.py:590
  25.5 0.8 %multiply_add_fusion.1 = f32[40,16,128]{2,1,0:T(8,128)} fusion(f32[40,16,128]{2,1,0:T(8,128)S(1)} %get-tuple-element.13, f32[16,128]{1,0:T(8,128)S(1)} %get-tuple-element.15, f32[40]{0:T(128)S(1)} %bitcast.4), kind=kLoop, calls=%fused_computation.1 | loop fusion | flops 163840 | bytes 663712 | tf_op jit(solution)/shard_map/add | solution.py:617
  26.3 0.0 copy-start
  26.4 1.1 %multiply_add_fusion = f32[64,32,128]{2,1,0:T(8,128)} fusion(f32[64,32,128]{2,1,0:T(8,128)S(1)} %get-tuple-element.10, f32[32,128]{1,0:T(8,128)S(1)} %get-tuple-element.12, f32[64]{0:T(128)S(1)} %bitcast.3), kind=kLoop, calls=%fused_computation | loop fusion | flops 524288 | bytes 2113792 | tf_op jit(solution)/shard_map/add | solution.py:616
  27.5 0.0 copy-done
  27.5 0.6 %broadcast_multiply_fusion = f32[4,8,128]{2,1,0:T(8,128)} fusion(f32[4,8,128]{2,1,0:T(8,128)S(1)} %get-tuple-element.16, f32[8,128]{1,0:T(8,128)S(1)} %convert_element_type.3), kind=kLoop, calls=%fused_computation.2 | loop fusion | flops 4096 | bytes 36864 | tf_op jit(solution)/shard_map/mul | solution.py:618
  (1 shorter events, 0.0 us)
Async XLA Ops:
  26.3 1.1 %copy-start = (s32[8,128]{1,0:T(8,128)S(1)}, s32[8,128]{1,0:T(8,128)}, u32[]{:S(2)}) copy-start(s32[8,128]{1,0:T(8,128)} %param.15) | copy-start | bytes 12292
